TPU v7x, 32 devices: a whole 2x2x4 slice. The times are simulated.
32 devices in a mesh: band: 8 (over z, y), domain: 4 (over x, core).
Axes of the slice: x: 2, y: 2, z: 4, core: 2. Of those that a mesh axis runs over, the one named last changes fastest.
Arguments:
- orbitals: bfloat16 [1024, 8, 5120], P('band', 'domain'), may hold values from -6 to 6
- boundary: bfloat16 [1024, 4, 5120], P('band'), may hold values from -6 to 6
- potential: bfloat16 [8, 5120], P('domain'), may hold values from 0 to 2
Outputs:
- correlation: float32 [1024, 1024], P('band', 'domain')
- projected: float32 [1024, 1024], P('band', 'domain')
All inputs are finite; a program needn't handle non-finite values.
Results may differ from a plain program's by a relative error of at most 0.0012.
Values may be sent and summed in bfloat16 or wider, within the bound.
A program may use at most 128 MiB of HBM per device.

v0:
```python
import jax
import jax.numpy as jnp
from jax import lax
from jax.sharding import PartitionSpec as P

NX = 160
NY = 32
NZ_DEV = 2
DEGREE = 4


filter_center = 5.5
filter_radius = 4.5


def padded_2(cells, sides, width):
    for axis, dim in sides:
        count = lax.axis_size(axis)
        ends = count - 1
        head = lax.slice_in_dim(cells, 0, width, axis=dim)
        tail = lax.slice_in_dim(cells, cells.shape[dim] - width, cells.shape[dim], axis=dim)
        cells = jnp.concatenate(
            [
                lax.ppermute(tail, axis, [(i, (i + 1) % count) for i in range(ends)]),
                cells,
                lax.ppermute(head, axis, [((i + 1) % count, i) for i in range(ends)]),
            ],
            axis=dim,
        )
    return cells


def second_diff(values, axis_pos):
    near = jnp.roll(values, 1, axis_pos) + jnp.roll(values, -1, axis_pos)
    far = jnp.roll(values, 2, axis_pos) + jnp.roll(values, -2, axis_pos)
    return (16.0 * near - far - 30.0 * values) / 12.0


def plane_part(values):
    shaped = values.reshape(values.shape[:-1] + (NY, NX))
    total = second_diff(shaped, -1) + second_diff(shaped, -2)
    return total.reshape(values.shape)


def hamiltonian(padded, potential):
    middle = padded[:, 2:-2]
    z_part = (
        16.0 * (padded[:, 1:-3] + padded[:, 3:-1])
        - (padded[:, :-4] + padded[:, 4:])
        - 30.0 * middle
    ) / 12.0
    laplace = z_part + plane_part(middle)
    return -0.5 * laplace + potential.astype(jnp.float32) * middle


def chebyshev(apply_ham, orb_block):
    earlier = orb_block
    current = (
        (apply_ham(orb_block) - filter_center * orb_block.astype(jnp.float32)) / filter_radius
    ).astype(jnp.bfloat16)
    for degree_step in range(DEGREE - 1):
        following = (
            2.0 * (apply_ham(current) - filter_center * current.astype(jnp.float32)) / filter_radius
        )
        following = (following - earlier.astype(jnp.float32)).astype(jnp.bfloat16)
        earlier, current = (current, following)
    return (current, apply_ham(current).astype(jnp.bfloat16))


def per_device(orbitals, boundary, potential):
    orb_count = orbitals.shape[0]
    domain_pos = lax.axis_index("domain")
    domain_count = lax.axis_size("domain")
    last_pos = domain_count - 1

    def apply_ham(values):
        padded = padded_2(values, (("domain", 1),), 2)
        lower_rim = jnp.where(domain_pos == 0, boundary[:, 0:2], padded[:, 0:2])
        upper_rim = jnp.where(domain_pos == last_pos, boundary[:, 2:4], padded[:, -2:])
        padded = jnp.concatenate([lower_rim, padded[:, 2:-2], upper_rim], axis=1).astype(
            jnp.float32
        )
        return hamiltonian(padded, potential)

    filtered, applied = chebyshev(apply_ham, orbitals)
    filtered = filtered.reshape(orb_count, -1)
    applied = applied.reshape(orb_count, -1)
    cell_y, cell_h = (
        lax.all_to_all(filtered, "band", split_axis=1, concat_axis=0, tiled=True),
        lax.all_to_all(applied, "band", split_axis=1, concat_axis=0, tiled=True),
    )
    cell_y, cell_h = (
        lax.all_gather(cell_y, "domain", axis=1, tiled=True),
        lax.all_gather(cell_h, "domain", axis=1, tiled=True),
    )
    column_count = cell_y.shape[0] // domain_count
    column_y = lax.dynamic_slice_in_dim(cell_y, domain_pos * column_count, column_count, 0)
    column_h = lax.dynamic_slice_in_dim(cell_h, domain_pos * column_count, column_count, 0)
    contract_dims = (((1,), (1,)), ((), ()))
    with_y = lax.dot_general(cell_y, column_y, contract_dims, preferred_element_type=jnp.float32)
    with_h = lax.dot_general(cell_y, column_h, contract_dims, preferred_element_type=jnp.float32)
    summed = lax.psum_scatter(
        jnp.concatenate([with_y, with_h], axis=1), "band", scatter_dimension=0, tiled=True
    )
    total_cells = NZ_DEV * NY * NX * domain_count
    correlation = summed[:, :column_count] / total_cells
    projected = summed[:, column_count:] / total_cells
    return (correlation, projected)


def solution(mesh):
    return jax.shard_map(
        per_device,
        mesh=mesh,
        in_specs=(P("band", "domain", None), P("band", None, None), P("domain", None)),
        out_specs=(P("band", "domain"), P("band", "domain")),
        check_vma=False,
    )
```

profile of v0, /device:TPU:0, one launch (start us, length us, event | category | flops | bytes accessed | tf_op | source)
XLA Modules:
  0.0 764.1 jit_solution(16479881715788332567)
XLA Ops:
  7.2 7.4 copy.8
  20.4 9.8 %fusion.114 = (bf16[128,2,5120]{2,1,0:T(2,128)(2,1)}, bf16[128,2,5120]{2,1,0:T(2,128)(2,1)}) fusion(bf16[128,4,5120]{2,1,0:T(4,128)(2,1)} %param.4), kind=kLoop, calls=%fused_computation.178 | loop fusion | bytes 10485760 | tf_op jit(solution)/shard_map/slice | solution.py:78
  30.2 6.1 copy.18
  36.3 7.5 copy.17
  49.8 5.4 copy-done
  55.6 5.0 fusion.106
  65.5 5.0 fusion.112
  77.6 19.4 %fusion.44 = (f32[128,2,32,160]{0,3,2,1:T(8,128)}, f32[128,2,32,160]{0,3,2,1:T(8,128)}) fusion(f32[128,2,32,159]{0,3,2,1:T(8,128)} %get-tuple-element.75, f32[128,2,32,1]{0,3,2,1:T(1,128)} %get-tuple-element.77, f32[128,2,32,1]{0,3,2,1:T(1,128)} %get-tuple-element.76, f32[128,2,32,159]{0,3,2,1:T(8,128)} %get-tuple-element.74, ...), kind=kLoop, calls=%fused_computation.66 | loop fusion | flops 20971520 | bytes 52428800 | tf_op jit(solution)/shard_map/sub | solution.py:36
  97.0 13.8 %fusion.2 = bf16[128,2,5120]{0,2,1:T(8,128)(2,1)S(1)} fusion(bf16[128,2,5120]{0,2,1:T(8,128)(2,1)} %copy.8, f32[128,6,5120]{0,2,1:T(8,128)} %copy-done, f32[128,2,32,160]{0,3,2,1:T(8,128)} %get-tuple-element.91, f32[128,2,32,160]{0,3,2,1:T(8,128)} %get-tuple-element.90, f32[2,5120]{1,0:T(2,128)S(1)} %convert_element_type.53), kind=kLoop, calls=%fused_computation.13 | loop fusion | flops 23592960 | bytes 41984000 | tf_op jit(solution)/shard_map/convert_element_type | solution.py:60
  110.8 8.7 %collective-permute-start.2 = (bf16[128,2,5120]{0,2,1:T(8,128)(2,1)S(1)}, bf16[128,2,5120]{0,2,1:T(8,128)(2,1)S(1)}, u32[]{:S(2)}, u32[]{:S(2)}) collective-permute-start(bf16[128,2,5120]{0,2,1:T(8,128)(2,1)S(1)} %fusion.2), channel_id=1, source_target_pairs={{0,1},{1,2},{2,3},{4,5},{5,6},{6,7},{8,9},{9,10},{10,11},{12,13},{... | collective-permute-start | bytes 7864328 | tf_op jit(solution)/shard_map/ppermute | solution.py:24
  128.9 5.4 copy-done.3
  134.6 5.0 fusion.98
  139.7 5.1 fusion.100
  144.8 5.1 fusion.104
  155.0 10.6 %fusion.48 = f32[128,2,32,160]{0,3,2,1:T(8,128)} fusion(f32[128,2,32,159]{0,3,2,1:T(8,128)} %get-tuple-element.59, f32[128,2,32,1]{0,3,2,1:T(1,128)S(1)} %get-tuple-element.61, f32[128,2,32,1]{0,3,2,1:T(1,128)S(1)} %get-tuple-element.60, f32[128,2,32,159]{0,3,2,1:T(8,128)} %get-tuple-element.58, f32[128,2,32,158]{0,3,2,1:T(8,128)} %get-tuple-element.55, ...), kind=kLoop, calls=%fused_computation.74 | loop fusion | flops 10485760 | bytes 26214400 | tf_op jit(solution)/shard_map/sub | solution.py:36
  165.6 11.2 %fusion.50 = f32[128,2,32,160]{0,3,2,1:T(8,128)} fusion(f32[128,2,31,160]{0,3,2,1:T(8,128)} %get-tuple-element.67, f32[128,2,1,160]{0,3,2,1:T(8,128)S(1)} %get-tuple-element.69, f32[128,2,1,160]{0,3,2,1:T(8,128)S(1)} %get-tuple-element.68, f32[128,2,31,160]{0,3,2,1:T(8,128)} %get-tuple-element.66, f32[128,2,30,160]{0,3,2,1:T(8,128)} %get-tuple-element.63, ...), kind=kLoop, calls=%fused_computation.78 | loop fusion | flops 10485760 | bytes 26214400 | tf_op jit(solution)/shard_map/sub | solution.py:36
  176.8 9.6 %fusion.3 = bf16[128,2,5120]{0,2,1:T(8,128)(2,1)} fusion(bf16[128,2,5120]{0,2,1:T(8,128)(2,1)} %copy.8, bf16[128,2,5120]{0,2,1:T(8,128)(2,1)} %copy-done.7, f32[128,6,5120]{0,2,1:T(8,128)S(1)} %bitcast.108, f32[128,2,32,160]{0,3,2,1:T(8,128)} %fusion.50, f32[128,2,32,160]{0,3,2,1:T(8,128)} %fusion.48, f32[2,5120]{1,0:T(2,128)S(1)} %convert_element_type.53), kind=kLoop, calls=%fused_computation.14 | loop fusion | flops 26214400 | bytes 44605440 | tf_op jit(solution)/shard_map/convert_element_type | solution.py:65
  186.4 28.7 %collective-permute-start.4 = (bf16[128,2,5120]{0,2,1:T(8,128)(2,1)}, bf16[128,2,5120]{0,2,1:T(8,128)(2,1)S(1)}, u32[]{:S(2)}, u32[]{:S(2)}) collective-permute-start(bf16[128,2,5120]{0,2,1:T(8,128)(2,1)} %fusion.3), channel_id=1, source_target_pairs={{0,1},{1,2},{2,3},{4,5},{5,6},{6,7},{8,9},{9,10},{10,11},{12,13},{... | collective-permute-start | bytes 7864328 | tf_op jit(solution)/shard_map/ppermute | solution.py:24
  223.7 5.4 copy-done.4
  229.5 5.0 fusion.90
  234.5 5.1 fusion.92
  239.7 5.1 fusion.96
  249.8 10.6 %fusion.52 = f32[128,2,32,160]{0,3,2,1:T(8,128)} fusion(f32[128,2,32,159]{0,3,2,1:T(8,128)} %get-tuple-element.43, f32[128,2,32,1]{0,3,2,1:T(1,128)S(1)} %get-tuple-element.45, f32[128,2,32,1]{0,3,2,1:T(1,128)S(1)} %get-tuple-element.44, f32[128,2,32,159]{0,3,2,1:T(8,128)} %get-tuple-element.42, f32[128,2,32,158]{0,3,2,1:T(8,128)} %get-tuple-element.39, ...), kind=kLoop, calls=%fused_computation.82 | loop fusion | flops 10485760 | bytes 26214400 | tf_op jit(solution)/shard_map/sub | solution.py:36
  260.5 11.2 %fusion.54 = f32[128,2,32,160]{0,3,2,1:T(8,128)} fusion(f32[128,2,31,160]{0,3,2,1:T(8,128)} %get-tuple-element.51, f32[128,2,1,160]{0,3,2,1:T(8,128)S(1)} %get-tuple-element.53, f32[128,2,1,160]{0,3,2,1:T(8,128)S(1)} %get-tuple-element.52, f32[128,2,31,160]{0,3,2,1:T(8,128)} %get-tuple-element.50, f32[128,2,30,160]{0,3,2,1:T(8,128)} %get-tuple-element.47, ...), kind=kLoop, calls=%fused_computation.86 | loop fusion | flops 10485760 | bytes 26214400 | tf_op jit(solution)/shard_map/sub | solution.py:36
  271.7 9.6 %fusion.6 = bf16[128,2,5120]{0,2,1:T(8,128)(2,1)} fusion(bf16[128,2,5120]{0,2,1:T(8,128)(2,1)} %copy-done.7, bf16[128,2,5120]{0,2,1:T(8,128)(2,1)} %fusion.3, f32[128,6,5120]{0,2,1:T(8,128)S(1)} %bitcast.110, f32[128,2,32,160]{0,3,2,1:T(8,128)} %fusion.54, f32[128,2,32,160]{0,3,2,1:T(8,128)} %fusion.52, f32[2,5120]{1,0:T(2,128)S(1)} %convert_element_type.53), kind=kLoop, calls=%fused_computation.17 | loop fusion | flops 26214400 | bytes 44605440 | tf_op jit(solution)/shard_map/convert_element_type | solution.py:65
  281.3 28.1 %collective-permute-start.6 = (bf16[128,2,5120]{0,2,1:T(8,128)(2,1)}, bf16[128,2,5120]{0,2,1:T(8,128)(2,1)S(1)}, u32[]{:S(2)}, u32[]{:S(2)}) collective-permute-start(bf16[128,2,5120]{0,2,1:T(8,128)(2,1)} %fusion.6), channel_id=1, source_target_pairs={{0,1},{1,2},{2,3},{4,5},{5,6},{6,7},{8,9},{9,10},{10,11},{12,13},{... | collective-permute-start | bytes 7864328 | tf_op jit(solution)/shard_map/ppermute | solution.py:24
  317.9 5.4 copy-done.2
  327.1 5.1 fusion.84
  332.3 5.1 fusion.88
  342.5 8.8 %fusion.56 = f32[128,2,32,160]{0,3,2,1:T(8,128)} fusion(f32[128,2,32,159]{0,3,2,1:T(8,128)} %get-tuple-element.27, f32[128,2,32,1]{0,3,2,1:T(1,128)S(1)} %get-tuple-element.29, f32[128,2,32,1]{0,3,2,1:T(1,128)S(1)} %get-tuple-element.28, f32[128,2,32,159]{0,3,2,1:T(8,128)} %get-tuple-element.26, f32[128,2,32,158]{0,3,2,1:T(8,128)} %get-tuple-element.23, ...), kind=kLoop, calls=%fused_computation.90 | loop fusion | flops 10485760 | bytes 26214400 | tf_op jit(solution)/shard_map/sub | solution.py:36
  351.3 11.2 %fusion.58 = f32[128,2,32,160]{0,3,2,1:T(8,128)} fusion(f32[128,2,31,160]{0,3,2,1:T(8,128)} %get-tuple-element.35, f32[128,2,1,160]{0,3,2,1:T(8,128)S(1)} %get-tuple-element.37, f32[128,2,1,160]{0,3,2,1:T(8,128)S(1)} %get-tuple-element.36, f32[128,2,31,160]{0,3,2,1:T(8,128)} %get-tuple-element.34, f32[128,2,30,160]{0,3,2,1:T(8,128)} %get-tuple-element.31, ...), kind=kLoop, calls=%fused_computation.94 | loop fusion | flops 10485760 | bytes 26214400 | tf_op jit(solution)/shard_map/sub | solution.py:36
  362.5 8.4 %fusion.9 = bf16[128,2,5120]{0,2,1:T(8,128)(2,1)} fusion(bf16[128,2,5120]{0,2,1:T(8,128)(2,1)S(1)} %copy-done.9, f32[128,6,5120]{0,2,1:T(8,128)S(1)} %bitcast.106, f32[128,2,32,160]{0,3,2,1:T(8,128)} %fusion.58, f32[128,2,32,160]{0,3,2,1:T(8,128)} %fusion.56, bf16[128,2,5120]{0,2,1:T(8,128)(2,1)} %fusion.6, f32[2,5120]{1,0:T(2,128)S(1)} %convert_element_type.53), kind=kLoop, calls=%fused_computation.20 | loop fusion | flops 26214400 | bytes 44605440 | tf_op jit(solution)/shard_map/convert_element_type | solution.py:65
  370.8 5.8 all-to-all-start
  376.7 29.1 %collective-permute-start.8 = (bf16[128,2,5120]{0,2,1:T(8,128)(2,1)}, bf16[128,2,5120]{0,2,1:T(8,128)(2,1)}, u32[]{:S(2)}, u32[]{:S(2)}) collective-permute-start(bf16[128,2,5120]{0,2,1:T(8,128)(2,1)} %fusion.9), channel_id=1, source_target_pairs={{0,1},{1,2},{2,3},{4,5},{5,6},{6,7},{8,9},{9,10},{10,11},{12,13},{... | collective-permute-start | bytes 7864328 | tf_op jit(solution)/shard_map/ppermute | solution.py:24
  405.8 11.6 %all-to-all-done = bf16[128,8,1280]{0,2,1:T(8,128)(2,1)} async-done(((bf16[128,8,1280]{0,2,1:T(8,128)(2,1)}), bf16[128,8,1280]{0,2,1:T(8,128)(2,1)}, u32[]{:S(2)}, u32[]{:S(2)}) %all-to-all-start) | async-done | bytes 2621472 | tf_op jit(solution)/shard_map/all_to_all | solution.py:89
  425.5 23.5 %collective-permute-done.9 = bf16[128,2,5120]{0,2,1:T(8,128)(2,1)S(1)} collective-permute-done((bf16[128,2,5120]{0,2,1:T(8,128)(2,1)}, bf16[128,2,5120]{0,2,1:T(8,128)(2,1)S(1)}, u32[]{:S(2)}, u32[]{:S(2)}) %collective-permute-start.9) | collective-permute-done | bytes 2621472 | tf_op jit(solution)/shard_map/ppermute | solution.py:26
  450.5 6.8 copy-done.1
  461.3 5.1 fusion.74
  466.4 8.6 %fusion.60 = f32[128,2,32,160]{0,3,2,1:T(8,128)} fusion(f32[128,2,32,159]{0,3,2,1:T(8,128)} %get-tuple-element.11, f32[128,2,32,1]{0,3,2,1:T(1,128)S(1)} %get-tuple-element.13, f32[128,2,32,1]{0,3,2,1:T(1,128)S(1)} %get-tuple-element.12, f32[128,2,32,159]{0,3,2,1:T(8,128)S(1)} %get-tuple-element.10, f32[128,2,32,158]{0,3,2,1:T(8,128)} %get-tuple-element.7, ...), kind=kLoop, calls=%fused_computation.98 | loop fusion | flops 10485760 | bytes 26214400 | tf_op jit(solution)/shard_map/sub | solution.py:36
  475.0 5.0 fusion.78
  480.1 5.6 fusion.80
  485.6 8.0 %fusion.62 = f32[128,2,32,160]{0,3,2,1:T(8,128)S(1)} fusion(f32[128,2,31,160]{0,3,2,1:T(8,128)} %get-tuple-element.19, f32[128,2,1,160]{0,3,2,1:T(8,128)S(1)} %get-tuple-element.21, f32[128,2,1,160]{0,3,2,1:T(8,128)S(1)} %get-tuple-element.20, f32[128,2,31,160]{0,3,2,1:T(8,128)} %get-tuple-element.18, f32[128,2,30,160]{0,3,2,1:T(8,128)} %get-tuple-element.15, ...), kind=kLoop, calls=%fused_computation.102 | loop fusion | flops 10485760 | bytes 26214400 | tf_op jit(solution)/shard_map/sub | solution.py:36
  494.9 5.3 fusion.15
  500.2 36.7 %all_to_all.38 = bf16[128,8,1280]{0,2,1:T(8,128)(2,1)S(1)} all-to-all(bf16[128,8,1280]{0,2,1:T(8,128)(2,1)S(1)} %bitcast.112), channel_id=1, replica_groups=mesh['band'=8,'domain'=4] {'band'}, dimensions={1} | all-to-all | bytes 5242880 | tf_op jit(solution)/shard_map/all_to_all | solution.py:90
  539.6 7.7 %fusion.70 = f32[1024,256]{0,1:T(8,128)S(1)} fusion(bf16[1024,5120]{1,0:T(8,128)(2,1)} %all-gather.3.cloned.1.call-done, s32[]{:T(128)S(6)} %select_n.60), kind=kOutput, calls=%fused_computation.121 | convolution fusion | flops 2684354560 | bytes 14155780 | tf_op jit(solution)/shard_map/dot_general | solution.py:100
  547.3 131.0 %all-gather.5.cloned.1.call-done = bf16[1024,5120]{1,0:T(8,128)(2,1)} async-done(((bf16[1024,1280]{1,0:T(8,128)(2,1)}), bf16[1024,5120]{1,0:T(8,128)(2,1)}) %all-gather.5.cloned.1.call-update) | async-done | bytes 10485776 | tf_op jit(solution)/shard_map/all_gather | solution.py:94
  678.3 6.4 fusion.68
  686.3 68.3 %reduce-scatter.2.cloned.1.call-done = f32[128,512]{0,1:T(8,128)} async-done(((f32[1024,512]{0,1:T(8,128)}), f32[128,512]{0,1:T(8,128)}) %reduce-scatter.2.cloned.1.call-update) | async-done | bytes 262160 | tf_op jit(solution)/shard_map/reduce_scatter | solution.py:102
  (133 shorter events, 91.7 us)
Async XLA Ops:
  14.6 29.2 %collective-permute-start.1 = (bf16[128,2,5120]{0,2,1:T(8,128)(2,1)}, bf16[128,2,5120]{0,2,1:T(8,128)(2,1)}, u32[]{:S(2)}, u32[]{:S(2)}) collective-permute-start(bf16[128,2,5120]{0,2,1:T(8,128)(2,1)} %copy.8), channel_id=1, source_target_pairs={{1,0},{2,1},{3,2},{5,4},{6,5},{7,6},{9,8},{10,9},{11,10},{13,12},{... | collective-permute-start | bytes 7864328 | tf_op jit(solution)/shard_map/ppermute | solution.py:26
  15.9 30.1 %collective-permute-start = (bf16[128,2,5120]{0,2,1:T(8,128)(2,1)}, bf16[128,2,5120]{0,2,1:T(8,128)(2,1)}, u32[]{:S(2)}, u32[]{:S(2)}) collective-permute-start(bf16[128,2,5120]{0,2,1:T(8,128)(2,1)} %copy.8), channel_id=1, source_target_pairs={{0,1},{1,2},{2,3},{4,5},{5,6},{6,7},{8,9},{9,10},{10,11},{12,13},{... | collective-permute-start | bytes 7864328 | tf_op jit(solution)/shard_map/ppermute | solution.py:24
  30.2 13.6 %copy-start.12 = (bf16[2,5120]{1,0:T(2,128)(2,1)S(1)}, bf16[2,5120]{1,0:T(2,128)(2,1)}, u32[]{:S(2)}) copy-start(bf16[2,5120]{1,0:T(2,128)(2,1)} %param.5) | copy-start | bytes 61444
  43.8 2.5 copy-start.5
  49.8 5.4 copy-start
  97.0 26.9 %copy-start.6 = (bf16[128,2,5120]{0,2,1:T(8,128)(2,1)S(1)}, bf16[128,2,5120]{0,2,1:T(8,128)(2,1)}, u32[]{:S(2)}) copy-start(bf16[128,2,5120]{0,2,1:T(8,128)(2,1)} %copy.17) | copy-start | bytes 7864324
  110.8 18.0 %copy-start.7 = (bf16[128,2,5120]{0,2,1:T(8,128)(2,1)}, bf16[128,2,5120]{0,2,1:T(8,128)(2,1)S(1)}, u32[]{:S(2)}) copy-start(bf16[128,2,5120]{0,2,1:T(8,128)(2,1)S(1)} %fusion.2) | copy-start | bytes 7864324
  110.8 13.1 %collective-permute-start.2 = (bf16[128,2,5120]{0,2,1:T(8,128)(2,1)S(1)}, bf16[128,2,5120]{0,2,1:T(8,128)(2,1)S(1)}, u32[]{:S(2)}, u32[]{:S(2)}) collective-permute-start(bf16[128,2,5120]{0,2,1:T(8,128)(2,1)S(1)} %fusion.2), channel_id=1, source_target_pairs={{0,1},{1,2},{2,3},{4,5},{5,6},{6,7},{8,9},{9,10},{10,11},{12,13},{... | collective-permute-start | bytes 7864328 | tf_op jit(solution)/shard_map/ppermute | solution.py:24
  119.6 7.8 %collective-permute-start.3 = (bf16[128,2,5120]{0,2,1:T(8,128)(2,1)S(1)}, bf16[128,2,5120]{0,2,1:T(8,128)(2,1)S(1)}, u32[]{:S(2)}, u32[]{:S(2)}) collective-permute-start(bf16[128,2,5120]{0,2,1:T(8,128)(2,1)S(1)} %fusion.2), channel_id=1, source_target_pairs={{1,0},{2,1},{3,2},{5,4},{6,5},{7,6},{9,8},{10,9},{11,10},{13,12},{... | collective-permute-start | bytes 7864328 | tf_op jit(solution)/shard_map/ppermute | solution.py:26
  128.8 5.4 copy-start.3
  155.0 21.8 %slice-start.8 = ((s8[15728640]{0:T(1024)(128)(4,1)}), s8[4194304]{0:T(1024)(128)(4,1)S(1)}, s32[]{:S(2)}) async-start(s8[15728640]{0:T(1024)(128)(4,1)} %bitcast.107), calls=%async_computation.14 | async-start | bytes 8388608
  155.0 21.8 %slice-start.9 = ((s8[15728640]{0:T(1024)(128)(4,1)}), s8[4194304]{0:T(1024)(128)(4,1)S(1)}, s32[]{:S(2)}) async-start(s8[15728640]{0:T(1024)(128)(4,1)} %bitcast.107), calls=%async_computation.15 | async-start | bytes 8388608
  155.0 21.8 %slice-start.10 = ((s8[15728640]{0:T(1024)(128)(4,1)}), s8[4194304]{0:T(1024)(128)(4,1)S(1)}, s32[]{:S(2)}) async-start(s8[15728640]{0:T(1024)(128)(4,1)} %bitcast.107), calls=%async_computation.16 | async-start | bytes 8388608
  165.6 11.2 %slice-start.11 = ((s8[15728640]{0:T(1024)(128)(4,1)}), s8[3145728]{0:T(1024)(128)(4,1)S(1)}, s32[]{:S(2)}) async-start(s8[15728640]{0:T(1024)(128)(4,1)} %bitcast.107), calls=%async_computation.17 | async-start | bytes 6291456
  186.4 33.3 %collective-permute-start.4 = (bf16[128,2,5120]{0,2,1:T(8,128)(2,1)}, bf16[128,2,5120]{0,2,1:T(8,128)(2,1)S(1)}, u32[]{:S(2)}, u32[]{:S(2)}) collective-permute-start(bf16[128,2,5120]{0,2,1:T(8,128)(2,1)} %fusion.3), channel_id=1, source_target_pairs={{0,1},{1,2},{2,3},{4,5},{5,6},{6,7},{8,9},{9,10},{10,11},{12,13},{... | collective-permute-start | bytes 7864328 | tf_op jit(solution)/shard_map/ppermute | solution.py:24
  215.1 7.0 collective-permute-start.5
  220.0 2.5 copy-start.8
  223.7 5.4 copy-start.4
  249.8 21.8 %slice-start.12 = ((s8[15728640]{0:T(1024)(128)(4,1)}), s8[4194304]{0:T(1024)(128)(4,1)S(1)}, s32[]{:S(2)}) async-start(s8[15728640]{0:T(1024)(128)(4,1)} %bitcast.109), calls=%async_computation.18 | async-start | bytes 8388608
  249.8 21.8 %slice-start.13 = ((s8[15728640]{0:T(1024)(128)(4,1)}), s8[4194304]{0:T(1024)(128)(4,1)S(1)}, s32[]{:S(2)}) async-start(s8[15728640]{0:T(1024)(128)(4,1)} %bitcast.109), calls=%async_computation.19 | async-start | bytes 8388608
  249.8 21.8 %slice-start.14 = ((s8[15728640]{0:T(1024)(128)(4,1)}), s8[4194304]{0:T(1024)(128)(4,1)S(1)}, s32[]{:S(2)}) async-start(s8[15728640]{0:T(1024)(128)(4,1)} %bitcast.109), calls=%async_computation.20 | async-start | bytes 8388608
  260.5 11.2 %slice-start.15 = ((s8[15728640]{0:T(1024)(128)(4,1)}), s8[3145728]{0:T(1024)(128)(4,1)S(1)}, s32[]{:S(2)}) async-start(s8[15728640]{0:T(1024)(128)(4,1)} %bitcast.109), calls=%async_computation.21 | async-start | bytes 6291456
  281.3 32.6 %collective-permute-start.6 = (bf16[128,2,5120]{0,2,1:T(8,128)(2,1)}, bf16[128,2,5120]{0,2,1:T(8,128)(2,1)S(1)}, u32[]{:S(2)}, u32[]{:S(2)}) collective-permute-start(bf16[128,2,5120]{0,2,1:T(8,128)(2,1)} %fusion.6), channel_id=1, source_target_pairs={{0,1},{1,2},{2,3},{4,5},{5,6},{6,7},{8,9},{9,10},{10,11},{12,13},{... | collective-permute-start | bytes 7864328 | tf_op jit(solution)/shard_map/ppermute | solution.py:24
  309.4 7.0 collective-permute-start.7
  314.2 2.5 copy-start.11
  317.9 5.4 copy-start.2
  342.4 20.0 %slice-start.4 = ((s8[15728640]{0:T(1024)(128)(4,1)}), s8[4194304]{0:T(1024)(128)(4,1)S(1)}, s32[]{:S(2)}) async-start(s8[15728640]{0:T(1024)(128)(4,1)} %bitcast.105), calls=%async_computation.10 | async-start | bytes 8388608
  342.5 20.0 %slice-start.5 = ((s8[15728640]{0:T(1024)(128)(4,1)}), s8[4194304]{0:T(1024)(128)(4,1)S(1)}, s32[]{:S(2)}) async-start(s8[15728640]{0:T(1024)(128)(4,1)} %bitcast.105), calls=%async_computation.11 | async-start | bytes 8388608
  342.5 20.0 %slice-start.6 = ((s8[15728640]{0:T(1024)(128)(4,1)}), s8[4194304]{0:T(1024)(128)(4,1)S(1)}, s32[]{:S(2)}) async-start(s8[15728640]{0:T(1024)(128)(4,1)} %bitcast.105), calls=%async_computation.12 | async-start | bytes 8388608
  351.3 11.2 %slice-start.7 = ((s8[15728640]{0:T(1024)(128)(4,1)}), s8[3145728]{0:T(1024)(128)(4,1)S(1)}, s32[]{:S(2)}) async-start(s8[15728640]{0:T(1024)(128)(4,1)} %bitcast.105), calls=%async_computation.13 | async-start | bytes 6291456
  351.3 11.2 %copy-start.9 = (bf16[128,2,5120]{0,2,1:T(8,128)(2,1)S(1)}, bf16[128,2,5120]{0,2,1:T(8,128)(2,1)}, u32[]{:S(2)}) copy-start(bf16[128,2,5120]{0,2,1:T(8,128)(2,1)} %fusion.3) | copy-start | bytes 7864324
  370.8 46.6 %all-to-all-start = ((bf16[128,8,1280]{0,2,1:T(8,128)(2,1)}), bf16[128,8,1280]{0,2,1:T(8,128)(2,1)}, u32[]{:S(2)}, u32[]{:S(2)}) async-start(bf16[128,8,1280]{0,2,1:T(8,128)(2,1)} %bitcast.111), calls=%async_computation | async-start | bytes 5242880 | tf_op jit(solution)/shard_map/all_to_all | solution.py:89
  376.7 162.9 %all-gather.3.cloned.1.call-start = ((), (), s32[]{:S(2)}) async-start(), calls=%async_computation.3 | async-start | bytes 13107200 | tf_op jit(solution)/shard_map/all_gather | solution.py:93
  376.7 46.7 %collective-permute-start.8 = (bf16[128,2,5120]{0,2,1:T(8,128)(2,1)}, bf16[128,2,5120]{0,2,1:T(8,128)(2,1)}, u32[]{:S(2)}, u32[]{:S(2)}) collective-permute-start(bf16[128,2,5120]{0,2,1:T(8,128)(2,1)} %fusion.9), channel_id=1, source_target_pairs={{0,1},{1,2},{2,3},{4,5},{5,6},{6,7},{8,9},{9,10},{10,11},{12,13},{... | collective-permute-start | bytes 7864328 | tf_op jit(solution)/shard_map/ppermute | solution.py:24
  421.8 256.5 %all-gather.5.cloned.1.call-start = ((), (), s32[]{:S(2)}) async-start(), calls=%async_computation.4 | async-start | bytes 13107200 | tf_op jit(solution)/shard_map/all_gather | solution.py:94
  421.9 27.1 %collective-permute-start.9 = (bf16[128,2,5120]{0,2,1:T(8,128)(2,1)}, bf16[128,2,5120]{0,2,1:T(8,128)(2,1)S(1)}, u32[]{:S(2)}, u32[]{:S(2)}) collective-permute-start(bf16[128,2,5120]{0,2,1:T(8,128)(2,1)} %fusion.9), channel_id=1, source_target_pairs={{1,0},{2,1},{3,2},{5,4},{6,5},{7,6},{9,8},{10,9},{11,10},{13,12},{... | collective-permute-start | bytes 7864328 | tf_op jit(solution)/shard_map/ppermute | solution.py:26
  425.5 23.8 %copy-start.10 = (bf16[128,2,5120]{0,2,1:T(8,128)(2,1)S(1)}, bf16[128,2,5120]{0,2,1:T(8,128)(2,1)}, u32[]{:S(2)}) copy-start(bf16[128,2,5120]{0,2,1:T(8,128)(2,1)} %fusion.9) | copy-start | bytes 7864324
  450.5 6.8 copy-start.1
  480.0 13.6 %slice-start = ((s8[15728640]{0:T(1024)(128)(4,1)}), s8[3145728]{0:T(1024)(128)(4,1)S(1)}, s32[]{:S(2)}) async-start(s8[15728640]{0:T(1024)(128)(4,1)} %bitcast.103), calls=%async_computation.6 | async-start | bytes 6291456
  480.0 13.6 %slice-start.1 = ((s8[15728640]{0:T(1024)(128)(4,1)}), s8[4194304]{0:T(1024)(128)(4,1)S(1)}, s32[]{:S(2)}) async-start(s8[15728640]{0:T(1024)(128)(4,1)} %bitcast.103), calls=%async_computation.7 | async-start | bytes 8388608
  485.6 8.0 %slice-start.2 = ((s8[15728640]{0:T(1024)(128)(4,1)}), s8[4194304]{0:T(1024)(128)(4,1)S(1)}, s32[]{:S(2)}) async-start(s8[15728640]{0:T(1024)(128)(4,1)} %bitcast.103), calls=%async_computation.8 | async-start | bytes 8388608
  485.6 9.2 %slice-start.3 = ((s8[15728640]{0:T(1024)(128)(4,1)}), s8[4194304]{0:T(1024)(128)(4,1)S(1)}, s32[]{:S(2)}) async-start(s8[15728640]{0:T(1024)(128)(4,1)} %bitcast.103), calls=%async_computation.9 | async-start | bytes 8388608
  539.5 215.1 %reduce-scatter.2.cloned.1.call-start = ((), (), s32[]{:S(2)}) async-start(), calls=%async_computation.5 | async-start | bytes 2359296 | tf_op jit(solution)/shard_map/reduce_scatter | solution.py:102
Sparse Core Ops, SparseCore 0:
  422.0 111.8 all-gather.2
  539.6 138.6 all-gather.4
  686.4 68.0 reduce-scatter.1
where the time goes:
time: 773 us; the launch traced here: 764 us
  waiting for transfers between devices  251 us (32%)
  local copies, waits for them, and re-layouts  172 us (22%)
  other arithmetic  163 us (21%)
  starting transfers between devices  113 us (15%)
  blocking collectives  36.7 us (5%)
  between operations  14.9 us (2%)
  matrix products  14.2 us (2%)
    all_gather x1, waiting for transfers between devices, per_device(): lax.all_gather(cell_h, 'domain', axis=1, tiled=True)  131 us
    sub x9, other arithmetic, second_diff(): return (16.0 * near - far - 30.0 * values) / 12.0  99.6 us
    ppermute x5, starting transfers between devices, padded_2(): lax.ppermute(tail, axis, [(i, (i + 1) % count) for i in range(ends)])  99.2 us
    reduce_scatter x1, waiting for transfers between devices, per_device(): lax.psum_scatter(jnp.concatenate([with_y, with_h], axis=1), 'band', scatt...  68.3 us
    unnamed x63, local copies, waits for them, and re-layouts  52.6 us
    slice x20, local copies, waits for them, and re-layouts, second_diff(): near = jnp.roll(values, 1, axis_pos) + jnp.roll(values, -1, axis_pos)  51.3 us
    slice x20, local copies, waits for them, and re-layouts, second_diff(): far = jnp.roll(values, 2, axis_pos) + jnp.roll(values, -2, axis_pos)  49.4 us
    all_to_all x1, blocking collectives, per_device(): lax.all_to_all(applied, 'band', split_axis=1, concat_axis=0, tiled=True)  36.7 us
  transfers between devices with their start and end apart: 14, of which 10 were waited for; matrix products, arithmetic and copies ran while one was open for 11% of the time, Pallas kernels for 0%

commit v1 on v0

--- a/solution.py
+++ b/solution.py
@@ -1,12 +1,20 @@
+import functools
+
 import jax
 import jax.numpy as jnp
 from jax import lax
+from jax.experimental import pallas as pl
+from jax.experimental.pallas import tpu as pltpu
 from jax.sharding import PartitionSpec as P
 
 NX = 160
 NY = 32
 NZ_DEV = 2
 DEGREE = 4
+LANES = 128
+PAD = 8
+YB = 8
+GAP = 2
 
 
 filter_center = 5.5
@@ -108,9 +116,196 @@
     return (correlation, projected)
 
 
+SCALE = 2.0 / filter_radius
+K_NEAR = SCALE * 16.0 / 24.0
+K_FAR = SCALE / 24.0
+
+
+def plane_in(src):
+    group = YB * NX
+    rows = jnp.concatenate(
+        [src[:, g * group : (g + 1) * group].astype(jnp.float32) for g in range(NY // YB)], axis=0
+    )
+    return rows.T.reshape(YB, NX, LANES)
+
+
+def fill_rims(buf, z):
+    for yi in range(YB):
+        buf[z, yi + GAP, PAD - 2 : PAD] = buf[z, yi + GAP, PAD + NX - 2 : PAD + NX]
+        buf[z, yi + GAP, PAD + NX : PAD + NX + 2] = buf[z, yi + GAP, PAD : PAD + 2]
+    turn = LANES // (NY // YB)
+    for k in range(GAP):
+        low = buf[z, YB + k, PAD : PAD + NX]
+        buf[z, k, PAD : PAD + NX] = pltpu.roll(low, turn, 1)
+        high = buf[z, GAP + k, PAD : PAD + NX]
+        buf[z, GAP + YB + k, PAD : PAD + NX] = pltpu.roll(high, LANES - turn, 1)
+
+
+def apply_step(cur, out, coef, kind, planes):
+    chunk = 40
+
+    @pl.loop(0, YB)
+    def _(yi):
+        for x0 in range(PAD, PAD + NX, chunk):
+            here = pl.ds(x0, chunk)
+            mids = [cur[z, yi + GAP, here] for z in range(planes + 4)]
+            for z in range(planes):
+                zc = z + 2
+                v = mids[zc]
+                near = (
+                    (mids[zc - 1] + mids[zc + 1])
+                    + (cur[zc, yi + 1, here] + cur[zc, yi + 3, here])
+                    + (cur[zc, yi + GAP, pl.ds(x0 - 1, chunk)] + cur[zc, yi + GAP, pl.ds(x0 + 1, chunk)])
+                )
+                far = (
+                    (mids[zc - 2] + mids[zc + 2])
+                    + (cur[zc, yi, here] + cur[zc, yi + 4, here])
+                    + (cur[zc, yi + GAP, pl.ds(x0 - 2, chunk)] + cur[zc, yi + GAP, pl.ds(x0 + 2, chunk)])
+                )
+                r = coef[z, yi, pl.ds(x0 - PAD, chunk)] * v - K_NEAR * near + K_FAR * far
+                if kind == "first":
+                    r = 0.5 * r
+                elif kind == "next":
+                    r = r - out[zc, yi + GAP, here]
+                else:
+                    r = r * (1.0 / SCALE) + filter_center * v
+                out[zc, yi + GAP, here] = r.astype(jnp.bfloat16).astype(jnp.float32)
+
+
+def filter_kernel(orb_ref, rim_ref, pot_ref, f_ref, a_ref, buf_a, buf_b, coef):
+    planes = orb_ref.shape[0]
+    count = orb_ref.shape[1]
+
+    for k in range(4):
+        z = k if k < 2 else planes + k
+        rim = plane_in(rim_ref[k])
+        buf_a[z, GAP : GAP + YB, PAD : PAD + NX] = rim
+        buf_b[z, GAP : GAP + YB, PAD : PAD + NX] = rim
+
+    @pl.loop(0, planes)
+    def _(z):
+        row = pot_ref[z].astype(jnp.float32)
+        spread = jnp.broadcast_to((row - 1.75) * SCALE, (count, row.shape[-1]))
+        coef[z] = plane_in(spread)
+        buf_a[z + 2, GAP : GAP + YB, PAD : PAD + NX] = plane_in(orb_ref[z])
+        fill_rims(buf_a, z + 2)
+
+    def rims(buf):
+        @pl.loop(0, planes)
+        def _(z):
+            fill_rims(buf, z + 2)
+
+    def emit(buf, ref):
+        @pl.loop(0, planes)
+        def _(z):
+            cells = buf[z + 2, GAP : GAP + YB, PAD : PAD + NX].reshape(YB * NX, LANES)
+            ref[z] = cells.T.astype(jnp.bfloat16)
+
+    cur, other = buf_a, buf_b
+    apply_step(cur, other, coef, "first", planes)
+    for _ in range(DEGREE - 1):
+        cur, other = other, cur
+        rims(cur)
+        apply_step(cur, other, coef, "next", planes)
+    cur, other = other, cur
+    rims(cur)
+    emit(cur, f_ref)
+    apply_step(cur, other, coef, "last", planes)
+    emit(other, a_ref)
+
+
+def run_filter(orb, rim, pot):
+    planes = orb.shape[0]
+    out = jax.ShapeDtypeStruct((planes, LANES, YB * NX), jnp.bfloat16)
+    whole = pl.BlockSpec(memory_space=pltpu.VMEM)
+    field = pltpu.VMEM((planes + 4, YB + 2 * GAP, NX + 2 * PAD, LANES), jnp.float32)
+    return pl.pallas_call(
+        filter_kernel,
+        out_shape=(out, out),
+        in_specs=[whole] * 3,
+        out_specs=(whole, whole),
+        scratch_shapes=[field, field, pltpu.VMEM((planes, YB, NX, LANES), jnp.float32)],
+        compiler_params=pltpu.CompilerParams(vmem_limit_bytes=56 * 1024 * 1024),
+        name="chebyshev",
+    )(orb, rim, pot[:, None])
+
+
+def gram_kernel(all_ref, f_ref, a_ref, out_ref):
+    parts, bands, groups, count, cells = all_ref.shape
+    rows = bands * count
+
+    @pl.loop(0, parts)
+    def _(d):
+        for ref, at in ((f_ref, 0), (a_ref, rows)):
+            total = jnp.zeros((rows, rows), jnp.float32)
+            for g in range(groups):
+                total += lax.dot_general(
+                    all_ref[d, :, g].reshape(rows, cells),
+                    ref[:, g].reshape(rows, cells),
+                    (((1,), (1,)), ((), ())),
+                    preferred_element_type=jnp.float32,
+                )
+            out_ref[:, d, :, at : at + rows] = total.reshape(bands, count, rows)
+
+
+def run_gram(everyone, own_f, own_a):
+    parts, bands, groups, count, cells = everyone.shape
+    whole = pl.BlockSpec(memory_space=pltpu.VMEM)
+    return pl.pallas_call(
+        gram_kernel,
+        out_shape=jax.ShapeDtypeStruct((bands, parts, count, 2 * bands * count), jnp.float32),
+        in_specs=[whole] * 3,
+        out_specs=whole,
+        compiler_params=pltpu.CompilerParams(vmem_limit_bytes=56 * 1024 * 1024),
+        name="gram",
+    )(everyone, own_f, own_a)
+
+
+def whole_orbitals(orbitals, boundary, potential):
+    orb_count, planes_here, plane = orbitals.shape
+    parts = lax.axis_size("domain")
+    bands = lax.axis_size("band")
+    part = lax.axis_index("domain")
+    count = orb_count // parts
+
+    split = orbitals.reshape(parts, count, planes_here, plane).transpose(0, 2, 1, 3)
+    mine = lax.all_to_all(split, "domain", split_axis=0, concat_axis=0, tiled=True)
+    mine = mine.reshape(parts * planes_here, count, plane)
+    rim = lax.dynamic_slice_in_dim(boundary, part * count, count, 0).transpose(1, 0, 2)
+    pot = lax.all_gather(potential, "domain", axis=0, tiled=True)
+    f, a = run_filter(mine, rim, pot)
+
+    groups = LANES // count
+    shape = (bands, groups, count, f.shape[-1])
+    f = lax.all_to_all(f, "band", split_axis=0, concat_axis=0, tiled=True).reshape(shape)
+    everyone = lax.all_gather(f, "domain", axis=0)
+    a = lax.all_to_all(a, "band", split_axis=0, concat_axis=0, tiled=True).reshape(shape)
+    partial = run_gram(everyone, f, a)
+    summed = lax.psum_scatter(
+        partial.reshape(bands * orb_count, -1), "band", scatter_dimension=0, tiled=True
+    )
+    total_cells = parts * planes_here * plane
+    summed = summed.reshape(orb_count, 2, parts, bands // parts, count) / total_cells
+    summed = lax.all_to_all(
+        summed.transpose(2, 1, 0, 3, 4), "domain", split_axis=0, concat_axis=0, tiled=True
+    )
+    summed = summed.transpose(1, 2, 3, 0, 4).reshape(2, orb_count, -1)
+    return summed[0], summed[1]
+
+
 def solution(mesh):
+    parts, bands = mesh.shape["domain"], mesh.shape["band"]
+
+    def body(orbitals, boundary, potential):
+        fits = (
+            orbitals.shape[0] * (NY // YB) == LANES * parts
+            and orbitals.shape[1] * parts == bands
+            and bands % parts == 0
+        )
+        return (whole_orbitals if fits else per_device)(orbitals, boundary, potential)
+
     return jax.shard_map(
-        per_device,
+        body,
         mesh=mesh,
         in_specs=(P("band", "domain", None), P("band", None, None), P("domain", None)),
         out_specs=(P("band", "domain"), P("band", "domain")),

time: 773 us -> 325 us (0.42); the launches traced: 764 us -> 324 us
  waiting for transfers between devices: 251 us -> 72 us
  other arithmetic: 163 us -> 0.97 us
  local copies, waits for them, and re-layouts: 172 us -> 15.5 us
  blocking collectives: 36.7 us -> 171 us
  starting transfers between devices: 113 us -> 4.38 us
  Pallas kernels: 0 us -> 46.3 us
  matrix products: 14.2 us -> 0 us
    all_gather x2 -> x1, waiting for transfers between devices: 131 us -> 3.69 us  [whole_orbitals(): everyone = lax.all_gather(f, 'domain', axis=0)]
    slice x46 -> x1, local copies, waits for them, and re-layouts: 112 us -> 0.02 us  [whole_orbitals(): return (summed[0], summed[1])]
    ppermute x10 -> x0, starting transfers between devices: 107 us -> none  [the longest x5 99.2 us: padded_2(): lax.ppermute(tail, axis, [(i, (i + 1) % count) for i in range(ends)])]
    all_to_all x1 -> x3, blocking collectives: 36.7 us -> 138 us  [the longest x1 66.7 us: whole_orbitals(): lax.all_to_all(f, 'band', split_axis=0, concat_axis=0, tiled=True)]
    sub x9 -> x0, other arithmetic: 99.6 us -> none  [second_diff(): return (16.0 * near - far - 30.0 * values) / 12.0]
    convert_element_type x11 -> x0, other arithmetic: 54.7 us -> none  [the longest x3 27.5 us: chebyshev(): following = (following - earlier.astype(jnp.float32)).astype(jnp.bfloat16)]
    unnamed x63 -> x9, local copies, waits for them, and re-layouts: 52.6 us -> 6.19 us
    pallas_call x0 -> x2, Pallas kernels: none -> 46.3 us  [the longest x1 33.3 us: run_filter(): pl.pallas_call(filter_kernel, out_shape=(out, out), in_specs=[whole] * 3,...]
  transfers between devices with their start and end apart: 14 -> 3, of which waited for: 10 -> 2; matrix products, arithmetic and copies ran while one was open for 11% -> 1% of each run, Pallas kernels for 0% -> 0%
where the time goes in v1:
time: 325 us; the launch traced here: 324 us
  blocking collectives  171 us (53%)
  waiting for transfers between devices  72 us (22%)
  Pallas kernels  46.3 us (14%)
  local copies, waits for them, and re-layouts  15.5 us (5%)
  between operations  14.1 us (4%)
  starting transfers between devices  4.38 us (1%)
    reduce_scatter x1, waiting for transfers between devices, whole_orbitals(): lax.psum_scatter(partial.reshape(bands * orb_count, -1), 'band', scatter_...  68.3 us
    all_to_all x1, blocking collectives, whole_orbitals(): lax.all_to_all(f, 'band', split_axis=0, concat_axis=0, tiled=True)  66.7 us
    all_to_all x1, blocking collectives, whole_orbitals(): lax.all_to_all(a, 'band', split_axis=0, concat_axis=0, tiled=True)  63.1 us
    pallas_call x1, Pallas kernels, run_filter(): pl.pallas_call(filter_kernel, out_shape=(out, out), in_specs=[whole] * 3,...  33.3 us
    all_gather x1, blocking collectives, whole_orbitals(): pot = lax.all_gather(potential, 'domain', axis=0, tiled=True)  32.6 us
    pallas_call x1, Pallas kernels, run_gram(): pl.pallas_call(gram_kernel, out_shape=jax.ShapeDtypeStruct((bands, parts,...  13 us
    all_to_all x1, blocking collectives, whole_orbitals(): lax.all_to_all(summed.transpose(2, 1, 0, 3, 4), 'domain', split_axis=0, c...  8.55 us
  transfers between devices with their start and end apart: 3, of which 2 were waited for; matrix products, arithmetic and copies ran while one was open for 1% of the time, Pallas kernels for 0%

profile of v1, /device:TPU:0, one launch (start us, length us, event | category | flops | bytes accessed | tf_op | source)
XLA Modules:
  0.0 324.1 jit_solution(8315393784009914366)
XLA Ops:
  7.2 3.9 %copy.28 = bf16[4,32,2,5120]{3,1,2,0:T(8,128)(2,1)} copy(bf16[4,32,2,5120]{3,2,1,0:T(2,128)(2,1)} %bitcast.28) | data formatting | bytes 5242880 | tf_op jit(solution)/shard_map/reshape | solution.py:271
  11.0 0.0 copy-start.2
  11.0 4.3 %all-to-all-start = ((bf16[4,2,32,5120]{3,2,1,0:T(8,128)(2,1)}), bf16[4,2,32,5120]{3,2,1,0:T(8,128)(2,1)S(1)}, u32[]{:S(2)}, u32[]{:S(2)}) async-start(bf16[4,2,32,5120]{3,2,1,0:T(8,128)(2,1)} %bitcast.25), calls=%async_computation | async-start | bytes 5242880 | tf_op jit(solution)/shard_map/all_to_all | solution.py:272
  15.4 0.0 all-gather.3.cloned.1.call-start
  15.4 0.0 copy-done.2
  15.4 32.6 %all-gather = bf16[4,2,5120]{2,1,0:T(2,128)(2,1)S(1)} all-gather(bf16[1,2,5120]{2,1,0:T(2,128)(2,1)S(1)} %bitcast.33), channel_id=1, replica_groups=mesh['band'=8,'domain'=4] {'domain'}, dimensions={0}, use_global_device_ids=true | all-gather | bytes 102400 | tf_op jit(solution)/shard_map/all_gather | solution.py:275
  48.0 0.7 broadcast_in_dim.4.pot_ref
  48.7 1.8 constant_dynamic-slice_fusion
  50.5 1.5 copy.29
  52.0 0.0 all-to-all-done
  52.0 0.0 copy-start
  52.0 1.5 copy-done
  53.5 33.3 %chebyshev.1 = (bf16[8,128,1280]{2,1,0:T(8,128)(2,1)}, bf16[8,128,1280]{2,1,0:T(8,128)(2,1)}) custom-call(bf16[8,32,5120]{2,1,0:T(8,128)(2,1)} %bitcast.24, bf16[4,32,5120]{2,1,0:T(8,128)(2,1)} %bitcast.27, bf16[8,1,5120]{2,1,0:T(2,128)(2,1)} %broadcast_in_dim.4.pot_ref), custom_call_target="tpu_custom_call" | custom-call | tf_op jit(solution)/shard_map/chebyshev/pallas_call | solution.py:222
  86.7 66.7 %all_to_all.20 = bf16[8,128,1280]{2,1,0:T(8,128)(2,1)} all-to-all(bf16[8,128,1280]{2,1,0:T(8,128)(2,1)} %get-tuple-element.4), channel_id=1, replica_groups=mesh['band'=8,'domain'=4] {'band'}, dimensions={0} | all-to-all | bytes 5242880 | tf_op jit(solution)/shard_map/all_to_all | solution.py:280
  153.5 0.0 copy-start.1
  153.5 0.0 all-gather.3.cloned.1.call-update
  153.5 0.0 reduce-scatter.2.cloned.1.call-start
  153.5 1.7 copy-done.1
  155.2 63.1 %all_to_all.21 = bf16[8,128,1280]{2,1,0:T(8,128)(2,1)} all-to-all(bf16[8,128,1280]{2,1,0:T(8,128)(2,1)S(1)} %copy-done.1), channel_id=1, replica_groups=mesh['band'=8,'domain'=4] {'band'}, dimensions={0} | all-to-all | bytes 5242880 | tf_op jit(solution)/shard_map/all_to_all | solution.py:282
  218.3 3.7 %all-gather.3.cloned.1.call-done.all_ref = bf16[4,8,4,32,1280]{4,3,2,1,0:T(8,128)(2,1)} async-done(((bf16[1,8,4,32,1280]{4,3,2,1,0:T(8,128)(2,1)}), bf16[4,8,4,32,1280]{4,3,2,1,0:T(8,128)(2,1)}) %all-gather.3.cloned.1.call-update) | async-done | bytes 10485776 | tf_op jit(solution)/shard_map/all_gather | solution.py:281
  222.0 13.0 %gram.1 = f32[8,4,32,512]{3,2,1,0:T(8,128)} custom-call(bf16[4,8,4,32,1280]{4,3,2,1,0:T(8,128)(2,1)} %all-gather.3.cloned.1.call-done.all_ref, bf16[8,4,32,1280]{3,2,1,0:T(8,128)(2,1)} %bitcast.22, bf16[8,4,32,1280]{3,2,1,0:T(8,128)(2,1)} %bitcast.23), custom_call_target="tpu_custom_call" | custom-call | tf_op jit(solution)/shard_map/gram/pallas_call | solution.py:254
  235.0 2.9 copy.19
  237.9 0.0 reduce-scatter.2.cloned.1.call-update
  237.9 68.3 %reduce-scatter.2.cloned.1.call-done = f32[128,512]{0,1:T(8,128)} async-done(((f32[1024,512]{0,1:T(8,128)}), f32[128,512]{0,1:T(8,128)}) %reduce-scatter.2.cloned.1.call-update) | async-done | bytes 262160 | tf_op jit(solution)/shard_map/reduce_scatter | solution.py:284
  306.2 1.0 broadcast_multiply_fusion
  307.2 8.5 %all_to_all.22 = f32[4,2,128,2,32]{2,4,3,1,0:T(8,128)S(1)} all-to-all(f32[4,2,128,2,32]{2,4,3,1,0:T(8,128)S(1)} %copy.20), channel_id=1, replica_groups=mesh['band'=8,'domain'=4] {'domain'}, dimensions={0} | all-to-all | bytes 524288 | tf_op jit(solution)/shard_map/all_to_all | solution.py:289
  315.8 0.8 copy.23
  316.5 0.8 copy.22
  (3 shorter events, 0.1 us)
Async XLA Ops:
  11.0 4.3 %copy-start.2 = (bf16[2,5120]{1,0:T(2,128)(2,1)S(1)}, bf16[2,5120]{1,0:T(2,128)(2,1)}, u32[]{:S(2)}) copy-start(bf16[2,5120]{1,0:T(2,128)(2,1)} %param.5) | copy-start | bytes 61444
  11.0 41.0 %all-to-all-start = ((bf16[4,2,32,5120]{3,2,1,0:T(8,128)(2,1)}), bf16[4,2,32,5120]{3,2,1,0:T(8,128)(2,1)S(1)}, u32[]{:S(2)}, u32[]{:S(2)}) async-start(bf16[4,2,32,5120]{3,2,1,0:T(8,128)(2,1)} %bitcast.25), calls=%async_computation | async-start | bytes 5242880 | tf_op jit(solution)/shard_map/all_to_all | solution.py:272
  15.4 206.6 %all-gather.3.cloned.1.call-start = ((), (), s32[]{:S(2)}) async-start(), calls=%async_computation.5 | async-start | bytes 13107200 | tf_op jit(solution)/shard_map/all_gather | solution.py:281
  52.0 1.5 copy-start
  153.5 1.7 copy-start.1
  153.5 152.7 %reduce-scatter.2.cloned.1.call-start = ((), (), s32[]{:S(2)}) async-start(), calls=%async_computation.6 | async-start | bytes 2359296 | tf_op jit(solution)/shard_map/reduce_scatter | solution.py:284
Sparse Core Ops, SparseCore 0:
  153.6 68.3 all-gather.2
  238.0 68.0 reduce-scatter.1

commit v2 on v1

--- a/solution.py
+++ b/solution.py
@@ -15,6 +15,7 @@
 PAD = 8
 YB = 8
 GAP = 2
+MESH = pl.DeviceIdType.MESH
 
 
 filter_center = 5.5
@@ -230,35 +231,208 @@
     )(orb, rim, pot[:, None])
 
 
-def gram_kernel(all_ref, f_ref, a_ref, out_ref):
-    parts, bands, groups, count, cells = all_ref.shape
+def meet_all(bands, parts, band, part):
+    barrier = pltpu.get_barrier_semaphore()
+    total = bands * parts
+    me = band * parts + part
+
+    @pl.loop(1, total)
+    def _(o):
+        t = lax.rem(me + o, total)
+        pl.semaphore_signal(
+            barrier, inc=1, device_id=(t // parts, lax.rem(t, parts)), device_id_type=MESH
+        )
+
+    pl.semaphore_wait(barrier, total - 1)
+
+
+def gram_kernel(
+    bands, parts, total_cells,
+    f_ref, a_ref, c_ref, p_ref,
+    all_f, own_a, blocks, landed,
+    f_send, f_recv, a_send, a_recv, x_send, mate_send, local_sem, b_send, b_recv,
+):
+    band, part = lax.axis_index("band"), lax.axis_index("domain")
+    lanes, cells = f_ref.shape[1:]
+    count = blocks.shape[2] // parts
+    groups = lanes // count
     rows = bands * count
+    wide = 2 * rows // parts
+    mate = part + 1 - 2 * lax.rem(part, 2)
+    across = lax.rem(part + 2, parts)
+    across_mate = lax.rem(mate + 2, parts)
+    meet_all(bands, parts, band, part)
+
+    def band_copy(src, dst, send, recv, o, incoming):
+        peer = lax.rem(band + o, bands)
+        source = lax.rem(band - o + bands, bands)
+        slot = source if incoming else band
+        return pltpu.make_async_remote_copy(
+            src_ref=src.at[peer], dst_ref=dst.at[slot], send_sem=send.at[o],
+            recv_sem=recv.at[slot], device_id=(peer, part), device_id_type=MESH,
+        )
+
+    def f_copy(o, incoming):
+        return band_copy(f_ref, all_f.at[part], f_send, f_recv.at[part], o, incoming)
+
+    def a_copy(o, incoming):
+        return band_copy(a_ref, own_a, a_send, a_recv, o, incoming)
+
+    def part_copy(owner, to, slot, send):
+        return pltpu.make_async_remote_copy(
+            src_ref=all_f.at[owner, slot], dst_ref=all_f.at[owner, slot], send_sem=send.at[slot],
+            recv_sem=f_recv.at[owner, slot], device_id=(band, to), device_id_type=MESH,
+        )
+
+    keep_f = pltpu.make_async_copy(f_ref.at[band], all_f.at[part, band], local_sem.at[0])
+    keep_a = pltpu.make_async_copy(a_ref.at[band], own_a.at[band], local_sem.at[1])
+    keep_f.start()
+    keep_a.start()
+
+    @pl.loop(1, bands)
+    def _(o):
+        f_copy(o, False).start()
+
+    keep_f.wait()
+    part_copy(part, across, band, x_send).start()
+    part_copy(part, mate, band, mate_send.at[0]).start()
+
+    @pl.loop(1, bands)
+    def _(o):
+        a_copy(o, False).start()
+
+    @pl.loop(1, bands)
+    def _(o):
+        slot = lax.rem(band - o + bands, bands)
+        f_copy(o, True).wait_recv()
+        part_copy(part, across, slot, x_send).start()
+        part_copy(part, mate, slot, mate_send.at[0]).start()
+
+    @pl.loop(0, bands)
+    def _(o):
+        slot = lax.rem(band - o + bands, bands)
+        part_copy(across, mate, slot, mate_send.at[1]).wait_recv()
+        part_copy(across, mate, slot, mate_send.at[1]).start()
+
+    keep_a.wait()
+
+    @pl.loop(1, bands)
+    def _(o):
+        a_copy(o, True).wait_recv()
+
+    def add_rows(owner):
+        total = jnp.zeros((rows, 2 * rows), jnp.float32)
+        for g in range(groups):
+            at = slice(g * count, (g + 1) * count)
+            sides = []
+            for k in range(parts):
+                two = slice(k * bands // parts, (k + 1) * bands // parts)
+                sides.append(all_f[part, two, at].reshape(wide // 2, cells))
+                sides.append(own_a[two, at].reshape(wide // 2, cells))
+            total += lax.dot_general(
+                all_f[owner, :, at].reshape(rows, cells),
+                jnp.concatenate(sides, axis=0),
+                (((1,), (1,)), ((), ())),
+                preferred_element_type=jnp.float32,
+            )
+        for k in range(parts):
+            blocks[:, k, pl.ds(pl.multiple_of(owner * count, count), count)] = total[
+                :, k * wide : (k + 1) * wide
+            ].reshape(bands, count, wide)
+
+    @pl.loop(0, bands)
+    def _(slot):
+        part_copy(mate, part, slot, mate_send.at[0]).wait_recv()
+        part_copy(across_mate, part, slot, mate_send.at[1]).wait_recv()
 
     @pl.loop(0, parts)
-    def _(d):
-        for ref, at in ((f_ref, 0), (a_ref, rows)):
-            total = jnp.zeros((rows, rows), jnp.float32)
-            for g in range(groups):
-                total += lax.dot_general(
-                    all_ref[d, :, g].reshape(rows, cells),
-                    ref[:, g].reshape(rows, cells),
-                    (((1,), (1,)), ((), ())),
-                    preferred_element_type=jnp.float32,
-                )
-            out_ref[:, d, :, at : at + rows] = total.reshape(bands, count, rows)
-
-
-def run_gram(everyone, own_f, own_a):
-    parts, bands, groups, count, cells = everyone.shape
+    def _(k):
+        add_rows(k)
+
+    me = band * parts + part
+    total_devices = bands * parts
+
+    def block_copy(o, incoming):
+        t = lax.rem(me + o, total_devices)
+        source = lax.rem(me - o + total_devices, total_devices)
+        slot = source if incoming else me
+        return pltpu.make_async_remote_copy(
+            src_ref=blocks.at[t // parts, lax.rem(t, parts)], dst_ref=landed.at[slot],
+            send_sem=b_send.at[o], recv_sem=b_recv.at[slot],
+            device_id=(t // parts, lax.rem(t, parts)), device_id_type=MESH,
+        )
+
+    @pl.loop(1, total_devices)
+    def _(o):
+        block_copy(o, False).start()
+
+    keep = pltpu.make_async_copy(blocks.at[band, part], landed.at[me], local_sem.at[0])
+    keep.start()
+    keep.wait()
+
+    @pl.loop(1, total_devices)
+    def _(o):
+        block_copy(o, True).wait_recv()
+
+    sums = []
+    for d in range(parts):
+        total = landed[d]
+        for b in range(1, bands):
+            total = total + landed[b * parts + d]
+        sums.append(total * (1.0 / total_cells))
+    for ref, at in ((c_ref, 0), (p_ref, wide // 2)):
+        ref[...] = jnp.concatenate(
+            [
+                sums[d][:, at + j * count : at + (j + 1) * count]
+                for j in range(bands // parts)
+                for d in range(parts)
+            ],
+            axis=1,
+        )
+
+    @pl.loop(1, bands)
+    def _(o):
+        f_copy(o, False).wait_send()
+        a_copy(o, False).wait_send()
+
+    @pl.loop(0, bands)
+    def _(slot):
+        part_copy(part, across, slot, x_send).wait_send()
+        part_copy(part, mate, slot, mate_send.at[0]).wait_send()
+        part_copy(across, mate, slot, mate_send.at[1]).wait_send()
+
+    @pl.loop(1, total_devices)
+    def _(o):
+        block_copy(o, False).wait_send()
+
+
+def run_gram(f, a, bands, parts, total_cells):
+    lanes, cells = f.shape[1:]
+    count = lanes // (NY // YB)
+    orb_count = count * parts
+    wide = 2 * bands * count // parts
     whole = pl.BlockSpec(memory_space=pltpu.VMEM)
+    out = jax.ShapeDtypeStruct((orb_count, bands * orb_count // parts), jnp.float32)
+    dma = pltpu.SemaphoreType.DMA
     return pl.pallas_call(
-        gram_kernel,
-        out_shape=jax.ShapeDtypeStruct((bands, parts, count, 2 * bands * count), jnp.float32),
-        in_specs=[whole] * 3,
-        out_specs=whole,
-        compiler_params=pltpu.CompilerParams(vmem_limit_bytes=56 * 1024 * 1024),
+        functools.partial(gram_kernel, bands, parts, total_cells),
+        out_shape=(out, out),
+        in_specs=[whole] * 2,
+        out_specs=(whole, whole),
+        scratch_shapes=[
+            pltpu.VMEM((parts, bands, lanes, cells), jnp.bfloat16),
+            pltpu.VMEM((bands, lanes, cells), jnp.bfloat16),
+            pltpu.VMEM((bands, parts, orb_count, wide), jnp.float32),
+            pltpu.VMEM((bands * parts, orb_count, wide), jnp.float32),
+            dma((bands,)), dma((parts, bands)), dma((bands,)), dma((bands,)),
+            dma((bands,)), dma((2, bands)), dma((2,)),
+            dma((bands * parts,)), dma((bands * parts,)),
+        ],
+        compiler_params=pltpu.CompilerParams(
+            collective_id=0, has_side_effects=True, vmem_limit_bytes=56 * 1024 * 1024
+        ),
         name="gram",
-    )(everyone, own_f, own_a)
+    )(f, a)
 
 
 def whole_orbitals(orbitals, boundary, potential):
@@ -275,22 +449,7 @@
     pot = lax.all_gather(potential, "domain", axis=0, tiled=True)
     f, a = run_filter(mine, rim, pot)
 
-    groups = LANES // count
-    shape = (bands, groups, count, f.shape[-1])
-    f = lax.all_to_all(f, "band", split_axis=0, concat_axis=0, tiled=True).reshape(shape)
-    everyone = lax.all_gather(f, "domain", axis=0)
-    a = lax.all_to_all(a, "band", split_axis=0, concat_axis=0, tiled=True).reshape(shape)
-    partial = run_gram(everyone, f, a)
-    summed = lax.psum_scatter(
-        partial.reshape(bands * orb_count, -1), "band", scatter_dimension=0, tiled=True
-    )
-    total_cells = parts * planes_here * plane
-    summed = summed.reshape(orb_count, 2, parts, bands // parts, count) / total_cells
-    summed = lax.all_to_all(
-        summed.transpose(2, 1, 0, 3, 4), "domain", split_axis=0, concat_axis=0, tiled=True
-    )
-    summed = summed.transpose(1, 2, 3, 0, 4).reshape(2, orb_count, -1)
-    return summed[0], summed[1]
+    return run_gram(f, a, bands, parts, parts * planes_here * plane)
 
 
 def solution(mesh):
@@ -301,6 +460,7 @@
             orbitals.shape[0] * (NY // YB) == LANES * parts
             and orbitals.shape[1] * parts == bands
             and bands % parts == 0
+            and parts == 4
         )
         return (whole_orbitals if fits else per_device)(orbitals, boundary, potential)
 

time: 325 us -> 265 us (0.82)
  the two profiles are of different devices: /device:TPU:0 before, /device:TPU:31 now
where the time goes in v2:
time: 265 us
  Pallas kernels  216 us (82%)
  blocking collectives  31.1 us (12%)
  local copies, waits for them, and re-layouts  12.5 us (5%)
  starting transfers between devices  4.6 us (2%)
    pallas_call x1, Pallas kernels, run_gram(): pl.pallas_call(functools.partial(gram_kernel, bands, parts, total_cells),...  183 us
    pallas_call x1, Pallas kernels, run_filter(): pl.pallas_call(filter_kernel, out_shape=(out, out), in_specs=[whole] * 3,...  33.2 us
    all_gather x1, blocking collectives, whole_orbitals(): pot = lax.all_gather(potential, 'domain', axis=0, tiled=True)  31.1 us
    unnamed x7, local copies, waits for them, and re-layouts  6.18 us
  transfers between devices with their start and end apart: 1, of which 0 were waited for; matrix products, arithmetic and copies ran while one was open for 2% of the time, Pallas kernels for 0%

profile of v2, /device:TPU:31, one launch (start us, length us, event | category | flops | bytes accessed | tf_op | source)
XLA Modules:
  0.0 264.6 jit_solution(5912276571317838663)
XLA Ops:
  0.6 3.8 %copy.16 = bf16[4,32,2,5120]{3,1,2,0:T(8,128)(2,1)} copy(bf16[4,32,2,5120]{3,2,1,0:T(2,128)(2,1)} %bitcast.12) | data formatting | bytes 5242880 | tf_op jit(solution)/shard_map/reshape | solution.py:445
  4.5 0.0 copy-start.1
  4.5 4.6 %all-to-all-start = ((bf16[4,2,32,5120]{3,2,1,0:T(8,128)(2,1)}), bf16[4,2,32,5120]{3,2,1,0:T(8,128)(2,1)S(1)}, u32[]{:S(2)}, u32[]{:S(2)}) async-start(bf16[4,2,32,5120]{3,2,1,0:T(8,128)(2,1)} %bitcast.10), calls=%async_computation | async-start | bytes 5242880 | tf_op jit(solution)/shard_map/all_to_all | solution.py:446
  9.1 0.0 copy-done.1
  9.1 31.1 %all-gather = bf16[4,2,5120]{2,1,0:T(2,128)(2,1)S(1)} all-gather(bf16[1,2,5120]{2,1,0:T(2,128)(2,1)S(1)} %bitcast.13), channel_id=1, replica_groups=mesh['band'=8,'domain'=4] {'domain'}, dimensions={0}, use_global_device_ids=true | all-gather | bytes 102400 | tf_op jit(solution)/shard_map/all_gather | solution.py:449
  40.2 0.7 broadcast_in_dim.4.pot_ref
  40.9 1.8 constant_dynamic-slice_fusion
  42.7 1.5 copy.17
  44.2 0.0 all-to-all-done
  44.2 0.0 copy-start
  44.3 1.5 copy-done
  45.7 33.2 %chebyshev.1 = (bf16[8,128,1280]{2,1,0:T(8,128)(2,1)}, bf16[8,128,1280]{2,1,0:T(8,128)(2,1)}) custom-call(bf16[8,32,5120]{2,1,0:T(8,128)(2,1)} %bitcast.9, bf16[4,32,5120]{2,1,0:T(8,128)(2,1)} %bitcast.11, bf16[8,1,5120]{2,1,0:T(2,128)(2,1)} %broadcast_in_dim.4.pot_ref), custom_call_target="tpu_custom_call" | custom-call | tf_op jit(solution)/shard_map/chebyshev/pallas_call | solution.py:223
  78.9 182.6 %gram.1 = (f32[128,256]{1,0:T(8,128)}, f32[128,256]{1,0:T(8,128)}) custom-call(bf16[8,128,1280]{2,1,0:T(8,128)(2,1)} %get-tuple-element.4.f_ref, bf16[8,128,1280]{2,1,0:T(8,128)(2,1)} %get-tuple-element.5.a_ref), custom_call_target="tpu_custom_call" | custom-call | tf_op jit(solution)/shard_map/gram/pallas_call | solution.py:417
  261.5 1.6 copy.20
  263.0 1.6 copy.21
Async XLA Ops:
  4.5 4.6 %copy-start.1 = (bf16[2,5120]{1,0:T(2,128)(2,1)S(1)}, bf16[2,5120]{1,0:T(2,128)(2,1)}, u32[]{:S(2)}) copy-start(bf16[2,5120]{1,0:T(2,128)(2,1)} %param.5) | copy-start | bytes 61444
  4.5 39.8 %all-to-all-start = ((bf16[4,2,32,5120]{3,2,1,0:T(8,128)(2,1)}), bf16[4,2,32,5120]{3,2,1,0:T(8,128)(2,1)S(1)}, u32[]{:S(2)}, u32[]{:S(2)}) async-start(bf16[4,2,32,5120]{3,2,1,0:T(8,128)(2,1)} %bitcast.10), calls=%async_computation | async-start | bytes 5242880 | tf_op jit(solution)/shard_map/all_to_all | solution.py:446
  44.2 1.5 copy-start

commit v3 on v2

--- a/solution.py
+++ b/solution.py
@@ -263,20 +263,33 @@
     across_mate = lax.rem(mate + 2, parts)
     meet_all(bands, parts, band, part)
 
-    def band_copy(src, dst, send, recv, o, incoming):
+    core = lax.rem(part, 2)
+
+    def turned(o, total):
+        return o + core * (total - 2 * o)
+
+    def band_copy(src, dst, send, recv, o, incoming, rows_at=slice(None)):
+        o = turned(o, bands)
         peer = lax.rem(band + o, bands)
         source = lax.rem(band - o + bands, bands)
         slot = source if incoming else band
         return pltpu.make_async_remote_copy(
-            src_ref=src.at[peer], dst_ref=dst.at[slot], send_sem=send.at[o],
+            src_ref=src.at[peer, rows_at], dst_ref=dst.at[slot, rows_at], send_sem=send.at[o],
             recv_sem=recv.at[slot], device_id=(peer, part), device_id_type=MESH,
         )
 
-    def f_copy(o, incoming):
-        return band_copy(f_ref, all_f.at[part], f_send, f_recv.at[part], o, incoming)
-
-    def a_copy(o, incoming):
-        return band_copy(a_ref, own_a, a_send, a_recv, o, incoming)
+    def f_copy(o, incoming, rows_at=slice(None)):
+        return band_copy(f_ref, all_f.at[part], f_send, f_recv.at[part], o, incoming, rows_at)
+
+    def a_copy(o, incoming, rows_at=slice(None)):
+        return band_copy(a_ref, own_a, a_send, a_recv, o, incoming, rows_at)
+
+    def start_piece(copy, k):
+        g, o = k // (bands - 1), 1 + lax.rem(k, bands - 1)
+        copy(o, False, pl.ds(pl.multiple_of(g * count, count), count)).start()
+
+    def from_band(o):
+        return lax.rem(band - turned(o, bands) + bands, bands)
 
     def part_copy(owner, to, slot, send):
         return pltpu.make_async_remote_copy(
@@ -289,9 +302,9 @@
     keep_f.start()
     keep_a.start()
 
-    @pl.loop(1, bands)
-    def _(o):
-        f_copy(o, False).start()
+    @pl.loop(0, groups * (bands - 1))
+    def _(k):
+        start_piece(f_copy, k)
 
     keep_f.wait()
     part_copy(part, across, band, x_send).start()
@@ -299,18 +312,16 @@
 
     @pl.loop(1, bands)
     def _(o):
-        a_copy(o, False).start()
-
-    @pl.loop(1, bands)
-    def _(o):
-        slot = lax.rem(band - o + bands, bands)
+        slot = from_band(o)
         f_copy(o, True).wait_recv()
         part_copy(part, across, slot, x_send).start()
         part_copy(part, mate, slot, mate_send.at[0]).start()
+        for i in range(groups):
+            start_piece(a_copy, (o - 1) * groups + i)
 
     @pl.loop(0, bands)
     def _(o):
-        slot = lax.rem(band - o + bands, bands)
+        slot = lax.rem(from_band(o) + bands, bands)
         part_copy(across, mate, slot, mate_send.at[1]).wait_recv()
         part_copy(across, mate, slot, mate_send.at[1]).start()
 
@@ -353,6 +364,7 @@
     total_devices = bands * parts
 
     def block_copy(o, incoming):
+        o = turned(o, total_devices)
         t = lax.rem(me + o, total_devices)
         source = lax.rem(me - o + total_devices, total_devices)
         slot = source if incoming else me

time: 265 us -> 262 us (0.989)
  the two profiles are of different devices: /device:TPU:31 before, /device:TPU:0 now
where the time goes in v3:
time: 262 us
  Pallas kernels  212 us (81%)
  blocking collectives  32.6 us (12%)
  local copies, waits for them, and re-layouts  12.5 us (5%)
  starting transfers between devices  4.34 us (2%)
    pallas_call x1, Pallas kernels, run_gram(): pl.pallas_call(functools.partial(gram_kernel, bands, parts, total_cells),...  179 us
    pallas_call x1, Pallas kernels, run_filter(): pl.pallas_call(filter_kernel, out_shape=(out, out), in_specs=[whole] * 3,...  33.2 us
    all_gather x1, blocking collectives, whole_orbitals(): pot = lax.all_gather(potential, 'domain', axis=0, tiled=True)  32.6 us
    unnamed x7, local copies, waits for them, and re-layouts  6.18 us
  transfers between devices with their start and end apart: 1, of which 0 were waited for; matrix products, arithmetic and copies ran while one was open for 2% of the time, Pallas kernels for 0%

profile of v3, /device:TPU:0, one launch (start us, length us, event | category | flops | bytes accessed | tf_op | source)
XLA Modules:
  0.0 262.0 jit_solution(4538481930666612131)
XLA Ops:
  0.6 3.8 %copy.16 = bf16[4,32,2,5120]{3,1,2,0:T(8,128)(2,1)} copy(bf16[4,32,2,5120]{3,2,1,0:T(2,128)(2,1)} %bitcast.12) | data formatting | bytes 5242880 | tf_op jit(solution)/shard_map/reshape | solution.py:457
  4.5 0.0 copy-start.1
  4.5 4.3 %all-to-all-start = ((bf16[4,2,32,5120]{3,2,1,0:T(8,128)(2,1)}), bf16[4,2,32,5120]{3,2,1,0:T(8,128)(2,1)S(1)}, u32[]{:S(2)}, u32[]{:S(2)}) async-start(bf16[4,2,32,5120]{3,2,1,0:T(8,128)(2,1)} %bitcast.10), calls=%async_computation | async-start | bytes 5242880 | tf_op jit(solution)/shard_map/all_to_all | solution.py:458
  8.8 0.0 copy-done.1
  8.8 32.6 %all-gather = bf16[4,2,5120]{2,1,0:T(2,128)(2,1)S(1)} all-gather(bf16[1,2,5120]{2,1,0:T(2,128)(2,1)S(1)} %bitcast.13), channel_id=1, replica_groups=mesh['band'=8,'domain'=4] {'domain'}, dimensions={0}, use_global_device_ids=true | all-gather | bytes 102400 | tf_op jit(solution)/shard_map/all_gather | solution.py:461
  41.4 0.7 broadcast_in_dim.4.pot_ref
  42.2 1.8 constant_dynamic-slice_fusion
  43.9 1.5 copy.17
  45.5 0.0 all-to-all-done
  45.5 0.0 copy-start
  45.5 1.5 copy-done
  47.0 33.2 %chebyshev.1 = (bf16[8,128,1280]{2,1,0:T(8,128)(2,1)}, bf16[8,128,1280]{2,1,0:T(8,128)(2,1)}) custom-call(bf16[8,32,5120]{2,1,0:T(8,128)(2,1)} %bitcast.9, bf16[4,32,5120]{2,1,0:T(8,128)(2,1)} %bitcast.11, bf16[8,1,5120]{2,1,0:T(2,128)(2,1)} %broadcast_in_dim.4.pot_ref), custom_call_target="tpu_custom_call" | custom-call | tf_op jit(solution)/shard_map/chebyshev/pallas_call | solution.py:223
  80.1 178.7 %gram.1 = (f32[128,256]{1,0:T(8,128)}, f32[128,256]{1,0:T(8,128)}) custom-call(bf16[8,128,1280]{2,1,0:T(8,128)(2,1)} %get-tuple-element.4.f_ref, bf16[8,128,1280]{2,1,0:T(8,128)(2,1)} %get-tuple-element.5.a_ref), custom_call_target="tpu_custom_call" | custom-call | tf_op jit(solution)/shard_map/gram/pallas_call | solution.py:429
  258.8 1.6 copy.20
  260.4 1.6 copy.21
Async XLA Ops:
  4.5 4.3 %copy-start.1 = (bf16[2,5120]{1,0:T(2,128)(2,1)S(1)}, bf16[2,5120]{1,0:T(2,128)(2,1)}, u32[]{:S(2)}) copy-start(bf16[2,5120]{1,0:T(2,128)(2,1)} %param.5) | copy-start | bytes 61444
  4.5 41.0 %all-to-all-start = ((bf16[4,2,32,5120]{3,2,1,0:T(8,128)(2,1)}), bf16[4,2,32,5120]{3,2,1,0:T(8,128)(2,1)S(1)}, u32[]{:S(2)}, u32[]{:S(2)}) async-start(bf16[4,2,32,5120]{3,2,1,0:T(8,128)(2,1)} %bitcast.10), calls=%async_computation | async-start | bytes 5242880 | tf_op jit(solution)/shard_map/all_to_all | solution.py:458
  45.5 1.5 copy-start

commit v4 on v3

--- a/solution.py
+++ b/solution.py
@@ -254,10 +254,10 @@
 ):
     band, part = lax.axis_index("band"), lax.axis_index("domain")
     lanes, cells = f_ref.shape[1:]
-    count = blocks.shape[2] // parts
-    groups = lanes // count
+    groups = NY // YB
+    count = lanes // groups
     rows = bands * count
-    wide = 2 * rows // parts
+    wide = rows // parts
     mate = part + 1 - 2 * lax.rem(part, 2)
     across = lax.rem(part + 2, parts)
     across_mate = lax.rem(mate + 2, parts)
@@ -325,82 +325,90 @@
         part_copy(across, mate, slot, mate_send.at[1]).wait_recv()
         part_copy(across, mate, slot, mate_send.at[1]).start()
 
-    keep_a.wait()
-
-    @pl.loop(1, bands)
-    def _(o):
-        a_copy(o, True).wait_recv()
-
-    def add_rows(owner):
-        total = jnp.zeros((rows, 2 * rows), jnp.float32)
-        for g in range(groups):
-            at = slice(g * count, (g + 1) * count)
-            sides = []
-            for k in range(parts):
-                two = slice(k * bands // parts, (k + 1) * bands // parts)
-                sides.append(all_f[part, two, at].reshape(wide // 2, cells))
-                sides.append(own_a[two, at].reshape(wide // 2, cells))
-            total += lax.dot_general(
-                all_f[owner, :, at].reshape(rows, cells),
-                jnp.concatenate(sides, axis=0),
-                (((1,), (1,)), ((), ())),
-                preferred_element_type=jnp.float32,
-            )
-        for k in range(parts):
-            blocks[:, k, pl.ds(pl.multiple_of(owner * count, count), count)] = total[
-                :, k * wide : (k + 1) * wide
-            ].reshape(bands, count, wide)
-
     @pl.loop(0, bands)
     def _(slot):
         part_copy(mate, part, slot, mate_send.at[0]).wait_recv()
         part_copy(across_mate, part, slot, mate_send.at[1]).wait_recv()
 
-    @pl.loop(0, parts)
-    def _(k):
-        add_rows(k)
-
     me = band * parts + part
     total_devices = bands * parts
 
-    def block_copy(o, incoming):
+    def block_copy(m, o, incoming, rows_at=slice(None)):
         o = turned(o, total_devices)
         t = lax.rem(me + o, total_devices)
         source = lax.rem(me - o + total_devices, total_devices)
         slot = source if incoming else me
         return pltpu.make_async_remote_copy(
-            src_ref=blocks.at[t // parts, lax.rem(t, parts)], dst_ref=landed.at[slot],
-            send_sem=b_send.at[o], recv_sem=b_recv.at[slot],
+            src_ref=blocks.at[m, t // parts, lax.rem(t, parts), rows_at],
+            dst_ref=landed.at[m, slot, rows_at],
+            send_sem=b_send.at[m, o], recv_sem=b_recv.at[m, slot],
             device_id=(t // parts, lax.rem(t, parts)), device_id_type=MESH,
         )
 
-    @pl.loop(1, total_devices)
-    def _(o):
-        block_copy(o, False).start()
-
-    keep = pltpu.make_async_copy(blocks.at[band, part], landed.at[me], local_sem.at[0])
-    keep.start()
-    keep.wait()
-
-    @pl.loop(1, total_devices)
-    def _(o):
-        block_copy(o, True).wait_recv()
-
-    sums = []
-    for d in range(parts):
-        total = landed[d]
-        for b in range(1, bands):
-            total = total + landed[b * parts + d]
-        sums.append(total * (1.0 / total_cells))
-    for ref, at in ((c_ref, 0), (p_ref, wide // 2)):
-        ref[...] = jnp.concatenate(
-            [
-                sums[d][:, at + j * count : at + (j + 1) * count]
-                for j in range(bands // parts)
-                for d in range(parts)
-            ],
-            axis=1,
-        )
+    def product(owner, columns):
+        total = jnp.zeros((rows, rows), jnp.float32)
+        for g in range(groups):
+            at = slice(g * count, (g + 1) * count)
+            total += lax.dot_general(
+                all_f[owner, :, at].reshape(rows, cells),
+                columns[:, at].reshape(rows, cells),
+                (((1,), (1,)), ((), ())),
+                preferred_element_type=jnp.float32,
+            )
+        return total
+
+    def send_products(m, columns):
+        @pl.loop(0, parts // 2)
+        def _(p):
+            pair = [product(2 * p + h, columns) for h in range(2)]
+            at = pl.ds(pl.multiple_of(p * count, count), count)
+            for k in range(parts):
+                blocks[m, :, k, at] = jnp.concatenate(
+                    [t[:, k * wide : (k + 1) * wide] for t in pair], axis=1
+                ).reshape(bands, count, 2 * wide)
+
+            @pl.loop(1, total_devices)
+            def _(o):
+                block_copy(m, o, False, at).start()
+
+        keep = pltpu.make_async_copy(
+            blocks.at[m, band, part], landed.at[m, me], local_sem.at[0]
+        )
+        keep.start()
+        keep.wait()
+
+    def finish(m, ref):
+        @pl.loop(1, total_devices)
+        def _(o):
+            block_copy(m, o, True).wait_recv()
+
+        sums = []
+        for d in range(parts):
+            total = landed[m, d]
+            for b in range(1, bands):
+                total = total + landed[m, b * parts + d]
+            sums.append(total * (1.0 / total_cells))
+        for k in range(parts):
+            p, h = k // 2, k % 2
+            ref[k * count : (k + 1) * count] = jnp.concatenate(
+                [
+                    sums[d][p * count : (p + 1) * count, h * wide + j * count : h * wide + (j + 1) * count]
+                    for j in range(bands // parts)
+                    for d in range(parts)
+                ],
+                axis=1,
+            )
+
+    send_products(0, all_f.at[part])
+    keep_a.wait()
+
+    @pl.loop(1, bands)
+    def _(o):
+        a_copy(o, True).wait_recv()
+
+    send_products(1, own_a)
+    finish(0, c_ref)
+    finish(1, p_ref)
 
     @pl.loop(1, bands)
     def _(o):
@@ -415,14 +423,15 @@
 
     @pl.loop(1, total_devices)
     def _(o):
-        block_copy(o, False).wait_send()
+        block_copy(0, o, False).wait_send()
+        block_copy(1, o, False).wait_send()
 
 
 def run_gram(f, a, bands, parts, total_cells):
     lanes, cells = f.shape[1:]
     count = lanes // (NY // YB)
     orb_count = count * parts
-    wide = 2 * bands * count // parts
+    block = (orb_count // 2, 2 * bands * count // parts)
     whole = pl.BlockSpec(memory_space=pltpu.VMEM)
     out = jax.ShapeDtypeStruct((orb_count, bands * orb_count // parts), jnp.float32)
     dma = pltpu.SemaphoreType.DMA
@@ -434,11 +443,11 @@
         scratch_shapes=[
             pltpu.VMEM((parts, bands, lanes, cells), jnp.bfloat16),
             pltpu.VMEM((bands, lanes, cells), jnp.bfloat16),
-            pltpu.VMEM((bands, parts, orb_count, wide), jnp.float32),
-            pltpu.VMEM((bands * parts, orb_count, wide), jnp.float32),
+            pltpu.VMEM((2, bands, parts, *block), jnp.float32),
+            pltpu.VMEM((2, bands * parts, *block), jnp.float32),
             dma((bands,)), dma((parts, bands)), dma((bands,)), dma((bands,)),
             dma((bands,)), dma((2, bands)), dma((2,)),
-            dma((bands * parts,)), dma((bands * parts,)),
+            dma((2, bands * parts)), dma((2, bands * parts)),
         ],
         compiler_params=pltpu.CompilerParams(
             collective_id=0, has_side_effects=True, vmem_limit_bytes=56 * 1024 * 1024
@@ -458,6 +467,7 @@
     mine = lax.all_to_all(split, "domain", split_axis=0, concat_axis=0, tiled=True)
     mine = mine.reshape(parts * planes_here, count, plane)
     rim = lax.dynamic_slice_in_dim(boundary, part * count, count, 0).transpose(1, 0, 2)
+    rim, potential = lax.optimization_barrier((rim, potential))
     pot = lax.all_gather(potential, "domain", axis=0, tiled=True)
     f, a = run_filter(mine, rim, pot)
 

time: 262 us -> 252 us (0.962)
  Pallas kernels: 212 us -> 205 us
  blocking collectives: 32.6 us -> 29.3 us
    pallas_call x1, Pallas kernels: 179 us -> 172 us  [run_gram(): pl.pallas_call(functools.partial(gram_kernel, bands, parts, total_cells),...]
    all_gather x1, blocking collectives: 32.6 us -> 29.3 us  [whole_orbitals(): pot = lax.all_gather(potential, 'domain', axis=0, tiled=True)]
where the time goes in v4:
time: 252 us; the launch traced here: 251 us
  Pallas kernels  205 us (81%)
  blocking collectives  29.3 us (12%)
  local copies, waits for them, and re-layouts  12.5 us (5%)
  starting transfers between devices  4.21 us (2%)
    pallas_call x1, Pallas kernels, run_gram(): pl.pallas_call(functools.partial(gram_kernel, bands, parts, total_cells),...  172 us
    pallas_call x1, Pallas kernels, run_filter(): pl.pallas_call(filter_kernel, out_shape=(out, out), in_specs=[whole] * 3,...  33.2 us
    all_gather x1, blocking collectives, whole_orbitals(): pot = lax.all_gather(potential, 'domain', axis=0, tiled=True)  29.3 us
    unnamed x7, local copies, waits for them, and re-layouts  6.18 us
  transfers between devices with their start and end apart: 1, of which 0 were waited for; matrix products, arithmetic and copies ran while one was open for 2% of the time, Pallas kernels for 0%

profile of v4, /device:TPU:0, one launch (start us, length us, event | category | flops | bytes accessed | tf_op | source)
XLA Modules:
  0.0 251.4 jit_solution(4576655733503503687)
XLA Ops:
  0.6 3.8 %copy.16 = bf16[4,32,2,5120]{3,1,2,0:T(8,128)(2,1)} copy(bf16[4,32,2,5120]{3,2,1,0:T(2,128)(2,1)} %bitcast.12) | data formatting | bytes 5242880 | tf_op jit(solution)/shard_map/reshape | solution.py:466
  4.5 4.2 %all-to-all-start = ((bf16[4,2,32,5120]{3,2,1,0:T(8,128)(2,1)}), bf16[4,2,32,5120]{3,2,1,0:T(8,128)(2,1)S(1)}, u32[]{:S(2)}, u32[]{:S(2)}) async-start(bf16[4,2,32,5120]{3,2,1,0:T(8,128)(2,1)} %bitcast.10), calls=%async_computation | async-start | bytes 5242880 | tf_op jit(solution)/shard_map/all_to_all | solution.py:467
  8.7 0.0 copy-start.1
  8.7 1.8 constant_dynamic-slice_fusion
  10.5 1.5 copy.17
  12.0 0.0 copy-done.1
  12.0 29.3 %all-gather = bf16[4,2,5120]{2,1,0:T(2,128)(2,1)S(1)} all-gather(bf16[1,2,5120]{2,1,0:T(2,128)(2,1)S(1)} %bitcast.13), channel_id=1, replica_groups=mesh['band'=8,'domain'=4] {'domain'}, dimensions={0}, use_global_device_ids=true | all-gather | bytes 102400 | tf_op jit(solution)/shard_map/all_gather | solution.py:471
  41.3 0.7 broadcast_in_dim.4.pot_ref
  42.0 0.0 all-to-all-done
  42.0 0.0 copy-start
  42.0 1.5 copy-done
  43.5 33.2 %chebyshev.1 = (bf16[8,128,1280]{2,1,0:T(8,128)(2,1)}, bf16[8,128,1280]{2,1,0:T(8,128)(2,1)}) custom-call(bf16[8,32,5120]{2,1,0:T(8,128)(2,1)} %bitcast.9, bf16[4,32,5120]{2,1,0:T(8,128)(2,1)} %bitcast.11, bf16[8,1,5120]{2,1,0:T(2,128)(2,1)} %broadcast_in_dim.4.pot_ref), custom_call_target="tpu_custom_call" | custom-call | tf_op jit(solution)/shard_map/chebyshev/pallas_call | solution.py:223
  76.7 171.5 %gram.1 = (f32[128,256]{1,0:T(8,128)}, f32[128,256]{1,0:T(8,128)}) custom-call(bf16[8,128,1280]{2,1,0:T(8,128)(2,1)} %get-tuple-element.8.f_ref, bf16[8,128,1280]{2,1,0:T(8,128)(2,1)} %get-tuple-element.9.a_ref), custom_call_target="tpu_custom_call" | custom-call | tf_op jit(solution)/shard_map/gram/pallas_call | solution.py:438
  248.2 1.6 copy.20
  249.8 1.6 copy.21
Async XLA Ops:
  4.5 37.6 %all-to-all-start = ((bf16[4,2,32,5120]{3,2,1,0:T(8,128)(2,1)}), bf16[4,2,32,5120]{3,2,1,0:T(8,128)(2,1)S(1)}, u32[]{:S(2)}, u32[]{:S(2)}) async-start(bf16[4,2,32,5120]{3,2,1,0:T(8,128)(2,1)} %bitcast.10), calls=%async_computation | async-start | bytes 5242880 | tf_op jit(solution)/shard_map/all_to_all | solution.py:467
  8.7 3.3 %copy-start.1 = (bf16[2,5120]{1,0:T(2,128)(2,1)S(1)}, bf16[2,5120]{1,0:T(2,128)(2,1)}, u32[]{:S(2)}) copy-start(bf16[2,5120]{1,0:T(2,128)(2,1)} %param.5) | copy-start | bytes 61444
  42.0 1.5 copy-start

commit v5 on v4

--- a/solution.py
+++ b/solution.py
@@ -173,7 +173,14 @@
                 out[zc, yi + GAP, here] = r.astype(jnp.bfloat16).astype(jnp.float32)
 
 
-def filter_kernel(orb_ref, rim_ref, pot_ref, f_ref, a_ref, buf_a, buf_b, coef):
+def emit(buf, ref):
+    @pl.loop(0, ref.shape[0])
+    def _(z):
+        cells = buf[z + 2, GAP : GAP + YB, PAD : PAD + NX].reshape(YB * NX, LANES)
+        ref[z] = cells.T.astype(jnp.bfloat16)
+
+
+def run_filter(orb_ref, rim_ref, pot_ref, f_ref, buf_a, buf_b, coef):
     planes = orb_ref.shape[0]
     count = orb_ref.shape[1]
 
@@ -195,12 +202,6 @@
         @pl.loop(0, planes)
         def _(z):
             fill_rims(buf, z + 2)
-
-    def emit(buf, ref):
-        @pl.loop(0, planes)
-        def _(z):
-            cells = buf[z + 2, GAP : GAP + YB, PAD : PAD + NX].reshape(YB * NX, LANES)
-            ref[z] = cells.T.astype(jnp.bfloat16)
 
     cur, other = buf_a, buf_b
     apply_step(cur, other, coef, "first", planes)
@@ -211,28 +212,10 @@
     cur, other = other, cur
     rims(cur)
     emit(cur, f_ref)
-    apply_step(cur, other, coef, "last", planes)
-    emit(other, a_ref)
-
-
-def run_filter(orb, rim, pot):
-    planes = orb.shape[0]
-    out = jax.ShapeDtypeStruct((planes, LANES, YB * NX), jnp.bfloat16)
-    whole = pl.BlockSpec(memory_space=pltpu.VMEM)
-    field = pltpu.VMEM((planes + 4, YB + 2 * GAP, NX + 2 * PAD, LANES), jnp.float32)
-    return pl.pallas_call(
-        filter_kernel,
-        out_shape=(out, out),
-        in_specs=[whole] * 3,
-        out_specs=(whole, whole),
-        scratch_shapes=[field, field, pltpu.VMEM((planes, YB, NX, LANES), jnp.float32)],
-        compiler_params=pltpu.CompilerParams(vmem_limit_bytes=56 * 1024 * 1024),
-        name="chebyshev",
-    )(orb, rim, pot[:, None])
-
-
-def meet_all(bands, parts, band, part):
-    barrier = pltpu.get_barrier_semaphore()
+    return cur, other
+
+
+def greet_all(barrier, bands, parts, band, part):
     total = bands * parts
     me = band * parts + part
 
@@ -243,12 +226,11 @@
             barrier, inc=1, device_id=(t // parts, lax.rem(t, parts)), device_id_type=MESH
         )
 
-    pl.semaphore_wait(barrier, total - 1)
-
 
 def gram_kernel(
     bands, parts, total_cells,
-    f_ref, a_ref, c_ref, p_ref,
+    orb_ref, rim_ref, pot_ref, c_ref, p_ref,
+    buf_a, buf_b, coef, f_ref, a_ref,
     all_f, own_a, blocks, landed,
     f_send, f_recv, a_send, a_recv, x_send, mate_send, local_sem, b_send, b_recv,
 ):
@@ -261,7 +243,10 @@
     mate = part + 1 - 2 * lax.rem(part, 2)
     across = lax.rem(part + 2, parts)
     across_mate = lax.rem(mate + 2, parts)
-    meet_all(bands, parts, band, part)
+    barrier = pltpu.get_barrier_semaphore()
+    greet_all(barrier, bands, parts, band, part)
+    cur, other = run_filter(orb_ref, rim_ref, pot_ref, f_ref, buf_a, buf_b, coef)
+    pl.semaphore_wait(barrier, bands * parts - 1)
 
     core = lax.rem(part, 2)
 
@@ -298,9 +283,7 @@
         )
 
     keep_f = pltpu.make_async_copy(f_ref.at[band], all_f.at[part, band], local_sem.at[0])
-    keep_a = pltpu.make_async_copy(a_ref.at[band], own_a.at[band], local_sem.at[1])
     keep_f.start()
-    keep_a.start()
 
     @pl.loop(0, groups * (bands - 1))
     def _(k):
@@ -309,6 +292,11 @@
     keep_f.wait()
     part_copy(part, across, band, x_send).start()
     part_copy(part, mate, band, mate_send.at[0]).start()
+
+    apply_step(cur, other, coef, "last", bands)
+    emit(other, a_ref)
+    keep_a = pltpu.make_async_copy(a_ref.at[band], own_a.at[band], local_sem.at[1])
+    keep_a.start()
 
     @pl.loop(1, bands)
     def _(o):
@@ -427,20 +415,24 @@
         block_copy(1, o, False).wait_send()
 
 
-def run_gram(f, a, bands, parts, total_cells):
-    lanes, cells = f.shape[1:]
-    count = lanes // (NY // YB)
+def run_all(orb, rim, pot, bands, parts, total_cells):
+    planes, count = orb.shape[:2]
+    whole = pl.BlockSpec(memory_space=pltpu.VMEM)
+    dma = pltpu.SemaphoreType.DMA
+    lanes, cells = LANES, YB * NX
     orb_count = count * parts
     block = (orb_count // 2, 2 * bands * count // parts)
-    whole = pl.BlockSpec(memory_space=pltpu.VMEM)
+    field = pltpu.VMEM((planes + 4, YB + 2 * GAP, NX + 2 * PAD, LANES), jnp.float32)
+    pieces = pltpu.VMEM((planes, lanes, cells), jnp.bfloat16)
     out = jax.ShapeDtypeStruct((orb_count, bands * orb_count // parts), jnp.float32)
     dma = pltpu.SemaphoreType.DMA
     return pl.pallas_call(
         functools.partial(gram_kernel, bands, parts, total_cells),
         out_shape=(out, out),
-        in_specs=[whole] * 2,
+        in_specs=[whole] * 3,
         out_specs=(whole, whole),
         scratch_shapes=[
+            field, field, pltpu.VMEM((planes, YB, NX, LANES), jnp.float32), pieces, pieces,
             pltpu.VMEM((parts, bands, lanes, cells), jnp.bfloat16),
             pltpu.VMEM((bands, lanes, cells), jnp.bfloat16),
             pltpu.VMEM((2, bands, parts, *block), jnp.float32),
@@ -450,10 +442,10 @@
             dma((2, bands * parts)), dma((2, bands * parts)),
         ],
         compiler_params=pltpu.CompilerParams(
-            collective_id=0, has_side_effects=True, vmem_limit_bytes=56 * 1024 * 1024
+            collective_id=0, has_side_effects=True, vmem_limit_bytes=60 * 1024 * 1024
         ),
-        name="gram",
-    )(f, a)
+        name="filter_and_gram",
+    )(orb, rim, pot[:, None])
 
 
 def whole_orbitals(orbitals, boundary, potential):
@@ -469,9 +461,7 @@
     rim = lax.dynamic_slice_in_dim(boundary, part * count, count, 0).transpose(1, 0, 2)
     rim, potential = lax.optimization_barrier((rim, potential))
     pot = lax.all_gather(potential, "domain", axis=0, tiled=True)
-    f, a = run_filter(mine, rim, pot)
-
-    return run_gram(f, a, bands, parts, parts * planes_here * plane)
+    return run_all(mine, rim, pot, bands, parts, parts * planes_here * plane)
 
 
 def solution(mesh):

time: 252 us -> 240 us (0.952)
  Pallas kernels: 205 us -> 193 us
    pallas_call x2 -> x1, Pallas kernels: 205 us -> 193 us  [run_all(): pl.pallas_call(functools.partial(gram_kernel, bands, parts, total_cells),...]
where the time goes in v5:
time: 240 us; the launch traced here: 239 us
  Pallas kernels  193 us (80%)
  blocking collectives  29.4 us (12%)
  local copies, waits for them, and re-layouts  12.4 us (5%)
  starting transfers between devices  4.21 us (2%)
    pallas_call x1, Pallas kernels, run_all(): pl.pallas_call(functools.partial(gram_kernel, bands, parts, total_cells),...  193 us
    all_gather x1, blocking collectives, whole_orbitals(): pot = lax.all_gather(potential, 'domain', axis=0, tiled=True)  29.4 us
    unnamed x7, local copies, waits for them, and re-layouts  6.09 us
  transfers between devices with their start and end apart: 1, of which 0 were waited for; matrix products, arithmetic and copies ran while one was open for 2% of the time, Pallas kernels for 0%

profile of v5, /device:TPU:0, one launch (start us, length us, event | category | flops | bytes accessed | tf_op | source)
XLA Modules:
  0.0 239.3 jit_solution(3383659997174592718)
XLA Ops:
  0.6 3.8 %copy.16 = bf16[4,32,2,5120]{3,1,2,0:T(8,128)(2,1)} copy(bf16[4,32,2,5120]{3,2,1,0:T(2,128)(2,1)} %bitcast.12) | data formatting | bytes 5242880 | tf_op jit(solution)/shard_map/reshape | solution.py:458
  4.5 4.2 %all-to-all-start = ((bf16[4,2,32,5120]{3,2,1,0:T(8,128)(2,1)}), bf16[4,2,32,5120]{3,2,1,0:T(8,128)(2,1)S(1)}, u32[]{:S(2)}, u32[]{:S(2)}) async-start(bf16[4,2,32,5120]{3,2,1,0:T(8,128)(2,1)} %bitcast.10), calls=%async_computation | async-start | bytes 5242880 | tf_op jit(solution)/shard_map/all_to_all | solution.py:459
  8.7 0.0 copy-start.1
  8.7 1.8 constant_dynamic-slice_fusion
  10.4 1.5 copy.17
  11.9 0.0 copy-done.1
  11.9 29.4 %all-gather = bf16[4,2,5120]{2,1,0:T(2,128)(2,1)S(1)} all-gather(bf16[1,2,5120]{2,1,0:T(2,128)(2,1)S(1)} %bitcast.13), channel_id=1, replica_groups=mesh['band'=8,'domain'=4] {'domain'}, dimensions={0}, use_global_device_ids=true | all-gather | bytes 102400 | tf_op jit(solution)/shard_map/all_gather | solution.py:463
  41.3 0.8 broadcast_in_dim.4.pot_ref
  42.0 0.0 all-to-all-done
  42.0 0.0 copy-start
  42.0 1.5 copy-done
  43.5 192.6 %filter_and_gram.1 = (f32[128,256]{1,0:T(8,128)}, f32[128,256]{1,0:T(8,128)}) custom-call(bf16[8,32,5120]{2,1,0:T(8,128)(2,1)} %bitcast.9, bf16[4,32,5120]{2,1,0:T(8,128)(2,1)} %bitcast.11, bf16[8,1,5120]{2,1,0:T(2,128)(2,1)} %broadcast_in_dim.4.pot_ref), custom_call_target="tpu_custom_call" | custom-call | tf_op jit(solution)/shard_map/filter_and_gram/pallas_call | solution.py:429
  236.1 1.6 copy.20
  237.7 1.6 copy.21
Async XLA Ops:
  4.5 37.6 %all-to-all-start = ((bf16[4,2,32,5120]{3,2,1,0:T(8,128)(2,1)}), bf16[4,2,32,5120]{3,2,1,0:T(8,128)(2,1)S(1)}, u32[]{:S(2)}, u32[]{:S(2)}) async-start(bf16[4,2,32,5120]{3,2,1,0:T(8,128)(2,1)} %bitcast.10), calls=%async_computation | async-start | bytes 5242880 | tf_op jit(solution)/shard_map/all_to_all | solution.py:459
  8.7 3.2 %copy-start.1 = (bf16[2,5120]{1,0:T(2,128)(2,1)S(1)}, bf16[2,5120]{1,0:T(2,128)(2,1)}, u32[]{:S(2)}) copy-start(bf16[2,5120]{1,0:T(2,128)(2,1)} %param.5) | copy-start | bytes 61444
  42.0 1.5 copy-start

commit v6 on v5

--- a/solution.py
+++ b/solution.py
@@ -143,7 +143,7 @@
 
 
 def apply_step(cur, out, coef, kind, planes):
-    chunk = 40
+    chunk = 16
 
     @pl.loop(0, YB)
     def _(yi):

time: 240 us -> 239 us (level)
  no operation moved by 1% of the time
where the time goes in v6:
time: 239 us
  Pallas kernels  192 us (80%)
  blocking collectives  29.4 us (12%)
  local copies, waits for them, and re-layouts  12.4 us (5%)
  starting transfers between devices  4.21 us (2%)
    pallas_call x1, Pallas kernels, run_all(): pl.pallas_call(functools.partial(gram_kernel, bands, parts, total_cells),...  192 us
    all_gather x1, blocking collectives, whole_orbitals(): pot = lax.all_gather(potential, 'domain', axis=0, tiled=True)  29.4 us
    unnamed x7, local copies, waits for them, and re-layouts  6.09 us
  transfers between devices with their start and end apart: 1, of which 0 were waited for; matrix products, arithmetic and copies ran while one was open for 2% of the time, Pallas kernels for 0%

profile of v6, /device:TPU:0, one launch (start us, length us, event | category | flops | bytes accessed | tf_op | source)
XLA Modules:
  0.0 239.1 jit_solution(3577195141668341823)
XLA Ops:
  0.6 3.8 %copy.16 = bf16[4,32,2,5120]{3,1,2,0:T(8,128)(2,1)} copy(bf16[4,32,2,5120]{3,2,1,0:T(2,128)(2,1)} %bitcast.12) | data formatting | bytes 5242880 | tf_op jit(solution)/shard_map/reshape | solution.py:458
  4.5 4.2 %all-to-all-start = ((bf16[4,2,32,5120]{3,2,1,0:T(8,128)(2,1)}), bf16[4,2,32,5120]{3,2,1,0:T(8,128)(2,1)S(1)}, u32[]{:S(2)}, u32[]{:S(2)}) async-start(bf16[4,2,32,5120]{3,2,1,0:T(8,128)(2,1)} %bitcast.10), calls=%async_computation | async-start | bytes 5242880 | tf_op jit(solution)/shard_map/all_to_all | solution.py:459
  8.7 0.0 copy-start.1
  8.7 1.8 constant_dynamic-slice_fusion
  10.4 1.5 copy.17
  11.9 0.0 copy-done.1
  11.9 29.4 %all-gather = bf16[4,2,5120]{2,1,0:T(2,128)(2,1)S(1)} all-gather(bf16[1,2,5120]{2,1,0:T(2,128)(2,1)S(1)} %bitcast.13), channel_id=1, replica_groups=mesh['band'=8,'domain'=4] {'domain'}, dimensions={0}, use_global_device_ids=true | all-gather | bytes 102400 | tf_op jit(solution)/shard_map/all_gather | solution.py:463
  41.3 0.8 broadcast_in_dim.4.pot_ref
  42.0 0.0 all-to-all-done
  42.0 0.0 copy-start
  42.0 1.5 copy-done
  43.5 192.5 %filter_and_gram.1 = (f32[128,256]{1,0:T(8,128)}, f32[128,256]{1,0:T(8,128)}) custom-call(bf16[8,32,5120]{2,1,0:T(8,128)(2,1)} %bitcast.9, bf16[4,32,5120]{2,1,0:T(8,128)(2,1)} %bitcast.11, bf16[8,1,5120]{2,1,0:T(2,128)(2,1)} %broadcast_in_dim.4.pot_ref), custom_call_target="tpu_custom_call" | custom-call | tf_op jit(solution)/shard_map/filter_and_gram/pallas_call | solution.py:429
  236.0 1.6 copy.20
  237.6 1.6 copy.21
Async XLA Ops:
  4.5 37.6 %all-to-all-start = ((bf16[4,2,32,5120]{3,2,1,0:T(8,128)(2,1)}), bf16[4,2,32,5120]{3,2,1,0:T(8,128)(2,1)S(1)}, u32[]{:S(2)}, u32[]{:S(2)}) async-start(bf16[4,2,32,5120]{3,2,1,0:T(8,128)(2,1)} %bitcast.10), calls=%async_computation | async-start | bytes 5242880 | tf_op jit(solution)/shard_map/all_to_all | solution.py:459
  8.7 3.2 %copy-start.1 = (bf16[2,5120]{1,0:T(2,128)(2,1)S(1)}, bf16[2,5120]{1,0:T(2,128)(2,1)}, u32[]{:S(2)}) copy-start(bf16[2,5120]{1,0:T(2,128)(2,1)} %param.5) | copy-start | bytes 61444
  42.0 1.5 copy-start
